TPU v7x, 32 devices: a whole 2x2x4 slice. The times are simulated.
32 devices in a mesh: row: 4 (over x, core), col: 8 (over z, y).
Axes of the slice: x: 2, y: 2, z: 4, core: 2. Of those that a mesh axis runs over, the one named last changes fastest.
Arguments:
- basis: bfloat16 [576, 256, 128], P(('row', 'col')), may hold values from -1.5 to 1.5
- row_index: int32 [576, 128], P(('row', 'col')), may hold values from 0 to 255
- group_slot: int32 [576], P(('row', 'col')), may hold values from 0 to 767, as said below
- x_blocks: bfloat16 [48, 256, 256], P('row', 'col')
- zinv_blocks: bfloat16 [48, 256, 256], P('row', 'col')
Outputs:
- schur_tiles: float32 [48, 2048, 2048], P('row', None, 'col')
Inputs may be any that keep to these rules, and one draw needn't show every extreme that they name: Values are distinct; group_slot // 16 is the group's PSD block and group_slot % 16 its position there. A group stored on the device at (row index a, col index c) has its position among c * 2 to c * 2 + 1. Of the groups of one device, at most 5 belong to blocks of one index of row (blocks b with b // 12 equal to it), and every device reaches 5 for some index. The positions that the blocks of one index of row have on one index of col hold exactly 18 groups.
All inputs are finite; a program needn't handle non-finite values.
Results may differ from a plain program's by a relative error of at most 0.00048.
Values may be sent and summed in bfloat16 or wider, within the bound.
No kernel may reach another device: no remote copies, remote signals or barrier semaphores. Data moves between devices by JAX's collectives and lax.ppermute only.
A program may use at most 192 MiB of HBM per device.

v0:
```python
import jax
import jax.numpy as jnp
from jax import lax
from jax.sharding import PartitionSpec as P

GMAX = 16


def place_rows(selector, values):
    flat_values = values.reshape(values.shape[0], -1)
    moved_rows = jnp.dot(selector, flat_values, preferred_element_type=jnp.float32)
    return moved_rows.astype(values.dtype).reshape((selector.shape[0],) + values.shape[1:])


def place_ints(selector, values):
    moved_rows = jnp.dot(selector, values, preferred_element_type=jnp.int32)
    return moved_rows


def pair_tiles(members):
    stacked, x_full, z_full, rows_all, mask_all, near_basis, near_rows, near_mask = members
    group_width = near_basis.shape[-1]
    order = x_full.shape[0]
    positions = rows_all.shape[0]
    order_ids = jnp.arange(order, dtype=jnp.int32)
    row_pick = (rows_all.reshape(-1)[:, None] == order_ids[None, :]).astype(jnp.bfloat16)
    x_rows = (
        jnp.dot(row_pick, x_full, preferred_element_type=jnp.float32)
        .astype(jnp.bfloat16)
        .reshape(positions, group_width, order)
    )
    z_rows = (
        jnp.dot(row_pick, z_full, preferred_element_type=jnp.float32)
        .astype(jnp.bfloat16)
        .reshape(positions, group_width, order)
    )
    images = jnp.concatenate([stacked[:, 0], x_rows, stacked[:, 1], z_rows], axis=1)
    products = jnp.einsum("pcn,snk->pcsk", images, near_basis, preferred_element_type=jnp.float32)
    products = products.reshape(products.shape[0], products.shape[1], -1)
    column_pick = (order_ids[:, None] == near_rows.reshape(-1)[None, :]).astype(jnp.bfloat16)
    picked = jnp.einsum("pcn,nk->pck", images, column_pick, preferred_element_type=jnp.float32)
    upper = 2 * group_width
    third = 3 * group_width
    tile_sum = (
        products[:, group_width:upper] * picked[:, upper:third]
        + picked[:, group_width:upper] * products[:, upper:third]
    )
    tile_sum = (
        tile_sum
        + products[:, :group_width] * picked[:, third:]
        + picked[:, :group_width] * products[:, third:]
    )
    row_mask = mask_all.astype(jnp.float32)
    column_mask = jnp.repeat(near_mask.astype(jnp.float32), group_width)
    tile_sum = tile_sum * row_mask[:, None, None] * column_mask[None, None, :]
    return tile_sum.reshape(-1, tile_sum.shape[2])


def body(basis, row_index, group_slot, x_blocks, zinv_blocks):
    row_count = lax.axis_size("row")
    col_count = lax.axis_size("col")
    my_row = lax.axis_index("row")
    my_col = lax.axis_index("col")
    groups = basis.shape[0]
    owned = x_blocks.shape[0]
    places = GMAX // col_count
    capacity = (groups + row_count - 1) // row_count
    slot_count = row_count * capacity
    block_of = group_slot // GMAX
    owner_of = block_of // owned
    same_owner = (owner_of[:, None] == owner_of[None, :]).astype(jnp.int32)
    earlier = jnp.sum(jnp.tril(same_owner, -1), axis=1)
    target = owner_of * capacity + earlier
    choose = target[None, :] == jnp.arange(slot_count, dtype=jnp.int32)[:, None]
    send_basis = place_rows(choose.astype(jnp.bfloat16), basis)
    send_rows = place_ints(choose.astype(jnp.int32), row_index)
    send_slot = place_ints(choose.astype(jnp.int32), (group_slot + 1)[:, None])[:, 0] - 1
    got_basis, got_rows, got_slot = (
        lax.all_to_all(send_basis, "row", split_axis=0, concat_axis=0, tiled=True),
        lax.all_to_all(send_rows, "row", split_axis=0, concat_axis=0, tiled=True),
        lax.all_to_all(send_slot, "row", split_axis=0, concat_axis=0, tiled=True),
    )
    is_valid = got_slot >= 0
    spot_index = (got_slot // GMAX - my_row * owned) * places + (got_slot % GMAX - my_col * places)
    settle = (
        spot_index[None, :] == jnp.arange(owned * places, dtype=jnp.int32)[:, None]
    ) & is_valid[None, :]
    near_basis = place_rows(settle.astype(jnp.bfloat16), got_basis)
    near_basis = near_basis.reshape((owned, places) + near_basis.shape[1:])
    near_rows = place_ints(settle.astype(jnp.int32), got_rows).reshape(owned, places, -1)
    near_mask = (
        jnp.sum(settle.astype(jnp.float32), axis=1).astype(jnp.bfloat16).reshape(owned, places)
    )
    x_full, z_full, all_basis, rows_all, mask_all = (
        lax.all_gather(x_blocks, "col", axis=1, tiled=True),
        lax.all_gather(zinv_blocks, "col", axis=1, tiled=True),
        lax.all_gather(near_basis, "col", axis=1, tiled=True),
        lax.all_gather(near_rows, "col", axis=1, tiled=True),
        lax.all_gather(near_mask, "col", axis=1, tiled=True),
    )
    all_x = jnp.einsum(
        "jpnc,jnm->jpcm", all_basis, x_full, preferred_element_type=jnp.float32
    ).astype(jnp.bfloat16)
    all_z = jnp.einsum(
        "jpnc,jnm->jpcm", all_basis, z_full, preferred_element_type=jnp.float32
    ).astype(jnp.bfloat16)
    stacked = jnp.stack([all_x, all_z], axis=2)
    tile_blocks = lax.map(
        pair_tiles, (stacked, x_full, z_full, rows_all, mask_all, near_basis, near_rows, near_mask)
    )
    return tile_blocks


def solution(mesh):
    placed = (
        P(("row", "col"), None, None),
        P(("row", "col"), None),
        P(("row", "col")),
        P("row", "col", None),
        P("row", "col", None),
    )
    return jax.shard_map(
        body, mesh=mesh, in_specs=placed, out_specs=P("row", None, "col"), check_vma=False
    )
```

profile of v0, /device:TPU:0, one launch (start us, length us, event | category | flops | bytes accessed | tf_op | source)
XLA Modules:
  0.0 469.1 jit_solution(18264816812091439805)
XLA Ops:
  9.6 4.2 all-to-all-start
  18.4 3.6 all-to-all-start.1
  23.4 15.8 %all-to-all-done.1 = bf16[20,256,128]{2,1,0:T(8,128)(2,1)S(1)} async-done(((bf16[20,256,128]{2,1,0:T(8,128)(2,1)}), bf16[20,256,128]{2,1,0:T(8,128)(2,1)S(1)}, u32[]{:S(2)}, u32[]{:S(2)}) %all-to-all-start.1) | async-done | bytes 1310752 | tf_op jit(solution)/shard_map/all_to_all | solution.py:79
  44.5 3.2 all-to-all-start.2
  48.1 21.1 %all-gather = bf16[8,2,12]{2,1,0:T(2,128)(2,1)S(1)} all-gather(bf16[1,2,12]{2,1,0:T(2,128)(2,1)S(1)} %bitcast.139), channel_id=1, replica_groups=mesh['row'=4,'col'=8] {'col'}, dimensions={0}, use_global_device_ids=true | all-gather | bytes 432 | tf_op jit(solution)/shard_map/all_gather | solution.py:99
  69.5 31.7 %all_gather.18 = s32[12,16,128]{2,0,1:T(8,128)S(1)} all-gather(s32[12,2,128]{2,0,1:T(8,128)S(1)} %fusion.28), channel_id=1, replica_groups=mesh['row'=4,'col'=8] {'col'}, dimensions={1}, use_global_device_ids=true | all-gather | bytes 110592 | tf_op jit(solution)/shard_map/all_gather | solution.py:98
  101.2 133.9 %all-gather.5.cloned.1.call-done = bf16[12,16,256,128]{2,3,1,0:T(8,128)(2,1)} async-done(((bf16[12,2,256,128]{2,3,1,0:T(8,128)(2,1)}), bf16[12,16,256,128]{2,3,1,0:T(8,128)(2,1)}) %all-gather.5.cloned.1.call-update) | async-done | bytes 12582928 | tf_op jit(solution)/shard_map/all_gather | solution.py:97
  235.1 9.8 %convert_bitcast_fusion = bf16[12,16,1,128,256]{4,3,1,0,2:T(8,128)(2,1)} fusion(bf16[12,16,256,128]{2,3,1,0:T(8,128)(2,1)} %all-gather.5.cloned.1.call-done, bf16[12,256,256]{2,1,0:T(8,128)(2,1)} %all-gather.9.cloned.1.call-done), kind=kOutput, calls=%fused_computation.45 | convolution fusion | flops 3227516928 | bytes 26738688 | tf_op jit(solution)/shard_map/jpnc,jnm->jpcm/dot_general | solution.py:104
  244.9 34.8 %all-gather.7.cloned.1.call-done = bf16[12,256,256]{2,1,0:T(8,128)(2,1)} async-done(((bf16[12,32,256]{2,1,0:T(8,128)(2,1)}), bf16[12,256,256]{2,1,0:T(8,128)(2,1)}) %all-gather.7.cloned.1.call-update) | async-done | bytes 1572880 | tf_op jit(solution)/shard_map/all_gather | solution.py:95
  279.7 11.4 %convert_bitcast_fusion.1 = bf16[12,16,1,128,256]{4,3,1,0,2:T(8,128)(2,1)} fusion(bf16[12,16,256,128]{2,3,1,0:T(8,128)(2,1)} %all-gather.5.cloned.1.call-done, bf16[12,256,256]{2,1,0:T(8,128)(2,1)} %all-gather.7.cloned.1.call-done), kind=kOutput, calls=%fused_computation.46 | convolution fusion | flops 3227516928 | bytes 26738688 | tf_op jit(solution)/shard_map/jpnc,jnm->jpcm/dot_general | solution.py:101
  292.7 14.9 %pad_maximum_fusion.3 = bf16[12,16,2,128,256]{4,3,1,0,2:T(8,128)(2,1)} fusion(bf16[12,16,1,128,256]{4,3,1,0,2:T(8,128)(2,1)S(1)} %copy-done.2, bf16[12,16,1,128,256]{4,3,1,0,2:T(8,128)(2,1)} %convert_bitcast_fusion.1), kind=kLoop, calls=%fused_computation.44 | loop fusion | flops 12582912 | bytes 50331648 | tf_op jit(solution)/shard_map/stack | solution.py:107
  307.6 154.3 %while.10 = (s32[]{:T(128)}, f32[12,2048,256]{2,1,0:T(8,128)}, bf16[12,16,2,128,256]{4,3,1,0,2:T(8,128)(2,1)}, s32[12,16,128]{2,0,1:T(8,128)S(1)}, bf16[12,256,2...) while((s32[]{:T(128)}, f32[12,2048,256]{2,1,0:T(8,128)}, ...), condition=%wide.region_3.4_spmd, body=%wide.region_2.3_spmd.sunk | while | flops 2724790272 | bytes 59415352 | solution.py:108
  315.1 1.9 fusion.66
  317.1 1.9 fusion.70
  328.0 1.9 fusion.66
  330.0 1.9 fusion.70
  340.8 1.9 fusion.66
  342.9 1.9 fusion.70
  353.7 1.9 fusion.66
  355.7 1.9 fusion.70
  366.6 1.9 fusion.66
  379.4 1.9 fusion.66
  381.4 1.9 fusion.70
  392.3 1.9 fusion.66
  394.3 1.9 fusion.70
  405.1 1.9 fusion.66
  407.2 1.9 fusion.70
  418.0 1.9 fusion.66
  420.0 1.9 fusion.70
  430.9 1.9 fusion.66
  443.7 1.9 fusion.66
  456.6 1.9 fusion.66
  (193 shorter events, 133.0 us)
Async XLA Ops:
  6.5 37.3 %copy-start = (s32[18,128]{1,0:T(8,128)S(1)}, s32[18,128]{1,0:T(8,128)}, u32[]{:S(2)}) copy-start(s32[18,128]{1,0:T(8,128)} %param.8) | copy-start | bytes 27652
  6.5 94.7 %all-gather.9.cloned.1.call-start = ((), (), s32[]{:S(2)}) async-start(), calls=%async_computation.5 | async-start | bytes 1769472 | tf_op jit(solution)/shard_map/all_gather | solution.py:96
  9.6 8.8 %all-to-all-start = ((s32[4,5,1]{1,2,0:T(1,128)}), s32[4,5,1]{1,2,0:T(1,128)S(1)}, u32[]{:S(2)}, u32[]{:S(2)}) async-start(s32[4,5,1]{1,2,0:T(1,128)} %bitcast.20), calls=%async_computation | async-start | bytes 4096 | tf_op jit(solution)/shard_map/all_to_all | solution.py:81
  18.4 20.8 %all-to-all-start.1 = ((bf16[20,256,128]{2,1,0:T(8,128)(2,1)}), bf16[20,256,128]{2,1,0:T(8,128)(2,1)S(1)}, u32[]{:S(2)}, u32[]{:S(2)}) async-start(bf16[20,256,128]{2,1,0:T(8,128)(2,1)} %slice.40), calls=%async_computation.1 | async-start | bytes 2621440 | tf_op jit(solution)/shard_map/all_to_all | solution.py:79
  22.0 213.2 %all-gather.5.cloned.1.call-start = ((), (), s32[]{:S(2)}) async-start(), calls=%async_computation.3 | async-start | bytes 14155776 | tf_op jit(solution)/shard_map/all_gather | solution.py:97
  43.0 236.7 %all-gather.7.cloned.1.call-start = ((), (), s32[]{:S(2)}) async-start(), calls=%async_computation.4 | async-start | bytes 1769472 | tf_op jit(solution)/shard_map/all_gather | solution.py:95
  44.5 24.8 %all-to-all-start.2 = ((s32[4,5,128]{2,1,0:T(8,128)}), s32[4,5,128]{2,1,0:T(8,128)S(1)}, u32[]{:S(2)}, u32[]{:S(2)}) async-start(s32[4,5,128]{2,1,0:T(8,128)} %all_to_all.20), calls=%async_computation.2 | async-start | bytes 32768 | tf_op jit(solution)/shard_map/all_to_all | solution.py:80
  279.7 13.0 %copy-start.2 = (bf16[12,16,1,128,256]{4,3,1,0,2:T(8,128)(2,1)S(1)}, bf16[12,16,1,128,256]{4,3,1,0,2:T(8,128)(2,1)}, u32[]{:S(2)}) copy-start(bf16[12,16,1,128,256]{4,3,1,0,2:T(8,128)(2,1)} %convert_bitcast_fusion) | copy-start | bytes 37748740
  461.9 0.7 copy-start.1
Sparse Core Ops, SparseCore 0:
  9.5 46.9 all-gather.8
  58.7 176.3 all-gather.4
  237.3 42.3 all-gather.6
where the time goes:
time: 471 us; the launch traced here: 469 us
  waiting for transfers between devices  186 us (39%)
  matrix products  102 us (22%)
  local copies, waits for them, and re-layouts  64.7 us (14%)
  blocking collectives  52.8 us (11%)
  other arithmetic  39 us (8%)
  between operations  13.2 us (3%)
  starting transfers between devices  11.1 us (2%)
    all_gather x1, waiting for transfers between devices, body(): lax.all_gather(near_basis, 'col', axis=1, tiled=True)  134 us
    all_gather x1, waiting for transfers between devices, body(): lax.all_gather(x_blocks, 'col', axis=1, tiled=True)  34.8 us
    all_gather x1, blocking collectives, body(): lax.all_gather(near_rows, 'col', axis=1, tiled=True)  31.7 us
    dot_general x12, matrix products, pair_tiles(): jnp.einsum('pcn,snk->pcsk', images, near_basis, preferred_element_type=jn...  22.9 us
    mul x12, other arithmetic, pair_tiles(): tile_sum = tile_sum * row_mask[:, None, None] * column_mask[None, None, :]  22.2 us
    all_gather x1, blocking collectives, body(): lax.all_gather(near_mask, 'col', axis=1, tiled=True)  21.1 us
    squeeze x12, local copies, waits for them, and re-layouts, body(): lax.map(pair_tiles, (stacked, x_full, z_full, rows_all, mask_all, near_ba...  20.8 us
    dot_general x12, matrix products, pair_tiles(): jnp.dot(row_pick, x_full, preferred_element_type=jnp.float32)  20 us
  transfers between devices with their start and end apart: 6, of which 3 were waited for; matrix products, arithmetic and copies ran while one was open for 5% of the time, Pallas kernels for 0%

commit v1 on v0

v1 whole, which is shorter than its diff:
```python
import functools
import math

import jax
import jax.numpy as jnp
from jax import lax
from jax.experimental import pallas as pl
from jax.experimental.pallas import tpu as pltpu
from jax.sharding import PartitionSpec as P

GMAX = 16
LANES = 128
VMEM_LIMIT = 32 * 1024 * 1024
UNROLL = 3


def round_up(value, unit):
    return (value + unit - 1) // unit * unit


def ring_order(count):
    inner = max(d for d in range(1, math.isqrt(count) + 1) if count % d == 0)
    outer = count // inner
    path = []
    for line in range(outer):
        places = range(1, inner) if line % 2 == 0 else range(inner - 1, 0, -1)
        path += [line * inner + place for place in places]
    return path + [line * inner for line in range(outer - 1, -1, -1)]


def dot(left, right):
    return jnp.dot(left, right, preferred_element_type=jnp.float32)


def cost(groups, order, width, near, extra_bytes=0):
    steps = groups * width * order * (4 * order + 8 * near)
    moved = groups * width * (2 * order + 4 * near) + extra_bytes
    return pl.CostEstimate(flops=2 * steps, bytes_accessed=moved, transcendentals=0)


def whole(space=pltpu.VMEM):
    return pl.BlockSpec(memory_space=space)


def pack_kernel(dims, slot_ref, rows_ref, basis_ref, *refs):
    row_count, capacity, owned = dims
    outs = refs[:row_count]
    bins, notes, facts, counts, sems = refs[row_count:]
    groups, order, width = basis_ref.shape
    my_row = lax.axis_index("row")
    notes[...] = jnp.zeros_like(notes)
    facts[...] = jnp.zeros_like(facts)
    for shift in range(row_count):
        counts[shift] = 0
    lane = lax.broadcasted_iota(jnp.int32, (1, LANES), 1)

    def place(g, carry):
        slot = slot_ref[g]
        block = slot // GMAX
        owner = block // owned
        shift = lax.rem(owner - my_row + row_count, row_count)
        at = counts[shift]
        counts[shift] = at + 1
        start = pl.multiple_of(at * width, width)
        bins[shift, pl.ds(start, width), :] = basis_ref[g].T
        notes[shift, pl.ds(at, 1), :] = rows_ref[pl.ds(g, 1), :].astype(jnp.float32)
        fact = jnp.where(lane == 0, block - owner * owned + 1, 0)
        fact = jnp.where(lane == 1, slot - block * GMAX, fact)
        facts[shift, pl.ds(at, 1), :] = fact.astype(jnp.float32)
        return carry

    lax.fori_loop(0, groups, place, 0)
    copies = []
    for shift in range(row_count):
        bins[shift, capacity * width :, :width] = notes[shift].astype(jnp.bfloat16)
        bins[shift, capacity * width :, width : width + LANES] = facts[shift].astype(jnp.bfloat16)
        copies.append(pltpu.make_async_copy(bins.at[shift], outs[shift], sems.at[shift]))
        copies[-1].start()
    for copy in copies:
        copy.wait()


def pack(slots, rows, basis, row_count, capacity, owned):
    groups, order, width = basis.shape
    note_rows = round_up(capacity, 16)
    shape = (capacity * width + note_rows, order)
    return pl.pallas_call(
        functools.partial(pack_kernel, (row_count, capacity, owned)),
        out_shape=[jax.ShapeDtypeStruct(shape, jnp.bfloat16)] * row_count,
        in_specs=[whole(pltpu.SMEM), whole(), whole()],
        out_specs=[whole(pl.ANY)] * row_count,
        scratch_shapes=[
            pltpu.VMEM((row_count,) + shape, jnp.bfloat16),
            pltpu.VMEM((row_count, note_rows, width), jnp.float32),
            pltpu.VMEM((row_count, note_rows, LANES), jnp.float32),
            pltpu.SMEM((row_count,), jnp.int32),
            pltpu.SemaphoreType.DMA((row_count,)),
        ],
        compiler_params=pltpu.CompilerParams(vmem_limit_bytes=VMEM_LIMIT),
        name="pack",
    )(slots, rows, basis)


def compact_kernel(dims, *refs):
    row_count, capacity, groups, width, half, note_rows = dims
    bins = refs[:row_count]
    out, notes_in, notes, facts_in, facts, numbers, scalars, counts, sem = refs[row_count:]
    my_col = lax.axis_index("col")
    tail = capacity * width
    for shift in range(row_count):
        notes_in[shift] = bins[shift][tail:, :width].astype(jnp.float32)
        facts_in[shift] = bins[shift][tail:, width : width + LANES].astype(jnp.float32)
        numbers[shift] = facts_in[shift].astype(jnp.int32)
    copy = pltpu.make_async_copy(numbers, scalars, sem)
    copy.start()
    notes[...] = jnp.zeros_like(notes)
    facts[...] = jnp.zeros_like(facts)
    counts[0] = 0
    copy.wait()
    for shift in range(row_count):
        for k in range(capacity):

            @pl.when(scalars[shift, k, 0] > 0)
            def _():
                at = counts[0]
                counts[0] = at + 1
                start = at * width + jnp.where(at >= half, note_rows, 0)
                start = pl.multiple_of(start, 16)
                out[pl.ds(start, width), :] = bins[shift][k * width : (k + 1) * width, :]
                notes[pl.ds(at, 1), :] = notes_in[shift, k : k + 1, :]
                facts[pl.ds(at, 1), :] = facts_in[shift, k : k + 1, :]

    lane = lax.broadcasted_iota(jnp.int32, facts.shape, 1)
    marked = jnp.where(lane == 2, my_col.astype(jnp.float32), facts[...])
    middle = half * width
    out[middle : middle + note_rows, :width] = notes[...].astype(jnp.bfloat16)
    out[middle : middle + note_rows, width : width + LANES] = marked.astype(jnp.bfloat16)


def compact(bins, capacity, groups, width, half, note_rows):
    row_count = len(bins)
    order = bins[0].shape[1]
    bin_notes = bins[0].shape[0] - capacity * width
    return pl.pallas_call(
        functools.partial(compact_kernel, (row_count, capacity, groups, width, half, note_rows)),
        out_shape=jax.ShapeDtypeStruct((groups * width + note_rows, order), jnp.bfloat16),
        in_specs=[whole()] * row_count,
        out_specs=whole(),
        scratch_shapes=[
            pltpu.VMEM((row_count, bin_notes, width), jnp.float32),
            pltpu.VMEM((note_rows, width), jnp.float32),
            pltpu.VMEM((row_count, bin_notes, LANES), jnp.float32),
            pltpu.VMEM((note_rows, LANES), jnp.float32),
            pltpu.VMEM((row_count, bin_notes, LANES), jnp.int32),
            pltpu.SMEM((row_count, bin_notes, LANES), jnp.int32),
            pltpu.SMEM((1,), jnp.int32),
            pltpu.SemaphoreType.DMA,
        ],
        compiler_params=pltpu.CompilerParams(vmem_limit_bytes=VMEM_LIMIT),
        name="compact",
    )(*bins)


def read_notes(piece, start, note_rows, notes, facts, scalars, sem):
    width = notes.shape[1]
    notes[...] = piece[start : start + note_rows, :width].astype(jnp.float32)
    numbers = piece[start : start + note_rows, width : width + LANES].astype(jnp.float32)
    facts[...] = numbers.astype(jnp.int32)
    copy = pltpu.make_async_copy(facts, scalars, sem)
    copy.start()
    copy.wait()


def tiles_of(spans, dims, piece, notes, scalars, weights, out, stage, stage_sems):
    places, width = dims
    x_ref, z_ref, near_ref, pick_ref = weights
    order = x_ref.shape[1]
    slots = stage.shape[0]
    lane = lax.broadcasted_iota(jnp.int32, (width, order), 1).astype(jnp.float32)
    repeats = order // width

    def send(b, p, slot):
        start = pl.multiple_of(p * width, width)
        return pltpu.make_async_copy(
            stage.at[slot], out.at[b, pl.ds(start, width), :], stage_sems.at[slot]
        )

    def one(g, start, slot):
        b = scalars[g, 0] - 1
        p = scalars[g, 1]
        vectors = piece[pl.ds(start, width), :]
        turned = jnp.broadcast_to(notes[pl.ds(g, 1), :], (width, width)).T
        row_pick = (jnp.concatenate([turned] * repeats, axis=1) == lane).astype(jnp.bfloat16)
        left = jnp.concatenate([vectors, row_pick], axis=0)
        x_half = dot(left, x_ref[b]).astype(jnp.bfloat16)
        z_half = dot(left, z_ref[b]).astype(jnp.bfloat16)
        near, pick = near_ref[b], pick_ref[b]
        su_x, se_x = dot(x_half, near), dot(x_half, pick)
        su_z, se_z = dot(z_half, near), dot(z_half, pick)
        tile = su_x[width:] * se_z[:width] + se_x[width:] * su_z[:width]
        tile = tile + (su_x[:width] * se_z[width:] + se_x[:width] * su_z[width:])
        stage[slot] = tile
        send(b, p, slot).start()

    unroll = slots // 2
    rounds = 0
    for first, count, base in spans:
        whole_rounds = count // unroll

        def body(i, carry, first=first, base=base, rounds=rounds):
            bank = lax.rem(rounds + i, 2) * unroll

            @pl.when(rounds + i >= 2)
            def _():
                for k in range(unroll):
                    send(0, 0, bank + k).wait()

            for k in range(unroll):
                start = pl.multiple_of(base + (i * unroll + k) * width, 16)
                one(first + i * unroll + k, start, bank + k)
            return carry

        lax.fori_loop(0, whole_rounds, body, 0)
        rounds += whole_rounds
        rest = count - whole_rounds * unroll
        if rest:
            bank = rounds % 2 * unroll
            if rounds >= 2:
                for k in range(unroll):
                    send(0, 0, bank + k).wait()
            for k in range(rest):
                at = whole_rounds * unroll + k
                one(first + at, base + at * width, bank + k)
            for k in range(rest):
                send(0, 0, bank + k).wait()
            if rounds >= 1:
                for k in range(unroll):
                    send(0, 0, (unroll - bank) + k).wait()
            rounds = 0
    for last in range(max(rounds - 2, 0), rounds):
        for k in range(unroll):
            send(0, 0, last % 2 * unroll + k).wait()


def blank_tiles(groups, dims, scalars, flags, blank, out, sems):
    places, width = dims
    owned = out.shape[0]
    spots = owned * places

    def clear(s, carry):
        flags[s] = 0
        return carry

    def mark(g, carry):
        spot = (scalars[g, 0] - 1) * places + scalars[g, 1] - scalars[0, 2] * places
        flags[spot] = 1
        return carry

    def copy(s):
        b = s // places
        start = pl.multiple_of((scalars[0, 2] * places + s - b * places) * width, width)
        return pltpu.make_async_copy(blank, out.at[b, pl.ds(start, width), :], sems.at[s])

    def start(s, carry):
        @pl.when(flags[s] == 0)
        def _():
            copy(s).start()

        return carry

    def wait(s, carry):
        @pl.when(flags[s] == 0)
        def _():
            copy(s).wait()

        return carry

    lax.fori_loop(0, spots, clear, 0)
    lax.fori_loop(0, groups, mark, 0)
    lax.fori_loop(0, spots, start, 0)
    return lambda: lax.fori_loop(0, spots, wait, 0)


def first_kernel(dims, tables, *refs):
    groups, places, width, half, note_rows, parts, part = dims
    x_parts, z_parts = refs[:parts], refs[parts : 2 * parts]
    refs = refs[2 * parts :]
    piece, x_ref, z_ref, near_ref, pick_ref, out = refs[:6]
    notes, facts, scalars, near_rows, stage, blank = refs[6:12]
    flags, part_sems, note_sem, stage_sems, blank_sems = refs[12:]
    my_col = lax.axis_index("col")
    owned, order = x_ref.shape[:2]
    copies = []
    for side, (sources, ref, table) in enumerate(
        ((x_parts, x_ref, tables[0]), (z_parts, z_ref, tables[1]))
    ):
        for k in range(parts):
            col = jnp.int32(0)
            for c in range(parts):
                col = jnp.where(my_col == c, jnp.int32(table[c][k]), col)
            start = pl.multiple_of(col * part, part)
            copies.append(
                pltpu.make_async_copy(
                    sources[k], ref.at[:, pl.ds(start, part), :], part_sems.at[side * parts + k]
                )
            )
            copies[-1].start()
    blank[...] = jnp.zeros_like(blank)
    near_ref[...] = jnp.zeros_like(near_ref)
    near_rows[...] = jnp.full(near_rows.shape, -1.0, jnp.float32)
    read_notes(piece, half * width, note_rows, notes, facts, scalars, note_sem)
    blanks_done = blank_tiles(groups, (places, width), scalars, flags, blank, out, blank_sems)

    def settle(g, carry):
        b = scalars[g, 0] - 1
        place = scalars[g, 1] - my_col * places
        start = pl.multiple_of(g * width + jnp.where(g >= half, note_rows, 0), 16)
        turned = piece[pl.ds(start, width), :].T
        for k in range(places):

            @pl.when(place == k)
            def _():
                near_ref[b, :, k * width : (k + 1) * width] = turned
                near_rows[b, k : k + 1, :] = notes[pl.ds(g, 1), :]

        return carry

    lax.fori_loop(0, groups, settle, 0)
    deep = lax.broadcasted_iota(jnp.int32, (order, width), 0).astype(jnp.float32)

    def picks(b, carry):
        for k in range(places):
            hit = near_rows[b, k : k + 1, :] == deep
            pick_ref[b, :, k * width : (k + 1) * width] = hit.astype(jnp.bfloat16)
        return carry

    lax.fori_loop(0, owned, picks, 0)
    for copy in copies:
        copy.wait()
    spans = [(0, half, 0), (half, groups - half, half * width + note_rows)]
    weights = (x_ref, z_ref, near_ref, pick_ref)
    tiles_of(spans, (places, width), piece, notes, scalars, weights, out, stage, stage_sems)
    blanks_done()


def first_tiles(x_parts, z_parts, own, tables, sizes):
    groups, places, width, half, note_rows = sizes
    parts = len(x_parts)
    owned, part, order = x_parts[0].shape
    near = places * width
    square = jax.ShapeDtypeStruct((owned, order, order), jnp.bfloat16)
    narrow = jax.ShapeDtypeStruct((owned, order, near), jnp.bfloat16)
    out = jax.ShapeDtypeStruct((owned, GMAX * width, near), jnp.float32)
    return pl.pallas_call(
        functools.partial(
            first_kernel, (groups, places, width, half, note_rows, parts, part), tables
        ),
        out_shape=[square, square, narrow, narrow, out],
        in_specs=[whole(pl.ANY)] * (2 * parts) + [whole()],
        out_specs=[whole()] * 4 + [whole(pl.ANY)],
        scratch_shapes=[
            pltpu.VMEM((note_rows, width), jnp.float32),
            pltpu.VMEM((note_rows, LANES), jnp.int32),
            pltpu.SMEM((note_rows, LANES), jnp.int32),
            pltpu.VMEM((owned, round_up(places, 8), width), jnp.float32),
            pltpu.VMEM((2 * UNROLL, width, near), jnp.float32),
            pltpu.VMEM((width, near), jnp.float32),
            pltpu.SMEM((owned * places,), jnp.int32),
            pltpu.SemaphoreType.DMA((2 * parts,)),
            pltpu.SemaphoreType.DMA,
            pltpu.SemaphoreType.DMA((2 * UNROLL,)),
            pltpu.SemaphoreType.DMA((owned * places,)),
        ],
        cost_estimate=cost(groups, order, width, near),
        compiler_params=pltpu.CompilerParams(vmem_limit_bytes=VMEM_LIMIT),
        name="first_tiles",
    )(*x_parts, *z_parts, own)


def next_kernel(dims, plans, *refs):
    groups, places, width, note_rows = dims
    count = len(plans)
    pieces, weights = refs[:count], refs[count : count + 4]
    out, notes, facts, scalars, stage, blank = refs[count + 5 : count + 11]
    flags, note_sem, stage_sems, blank_sems = refs[count + 11 :]
    blank[...] = jnp.zeros_like(blank)
    for k, (note_start, spans, fills) in enumerate(plans):
        read_notes(pieces[k], note_start, note_rows, notes, facts, scalars, note_sem)
        if fills:
            blanks_done = blank_tiles(
                groups, (places, width), scalars, flags, blank, out, blank_sems
            )
        tiles_of(
            spans, (places, width), pieces[k], notes, scalars, weights, out, stage, stage_sems
        )
        if fills:
            blanks_done()


def next_tiles(pieces, plans, weights, out, sizes):
    groups, places, width, half, note_rows = sizes
    owned = out.shape[0]
    order = weights[0].shape[1]
    near = out.shape[2]
    count = len(pieces)
    return pl.pallas_call(
        functools.partial(next_kernel, (groups, places, width, note_rows), plans),
        out_shape=jax.ShapeDtypeStruct(out.shape, out.dtype),
        in_specs=[whole()] * (count + 4) + [whole(pl.ANY)],
        out_specs=whole(pl.ANY),
        input_output_aliases={count + 4: 0},
        scratch_shapes=[
            pltpu.VMEM((note_rows, width), jnp.float32),
            pltpu.VMEM((note_rows, LANES), jnp.int32),
            pltpu.SMEM((note_rows, LANES), jnp.int32),
            pltpu.VMEM((2 * UNROLL, width, near), jnp.float32),
            pltpu.VMEM((width, near), jnp.float32),
            pltpu.SMEM((owned * places,), jnp.int32),
            pltpu.SemaphoreType.DMA,
            pltpu.SemaphoreType.DMA((2 * UNROLL,)),
            pltpu.SemaphoreType.DMA((owned * places,)),
        ],
        cost_estimate=cost(
            sum(span[1] for plan in plans for span in plan[1]), order, width, near
        ),
        compiler_params=pltpu.CompilerParams(vmem_limit_bytes=VMEM_LIMIT),
        name="next_tiles",
    )(*pieces, *weights, out)


def body(basis, row_index, group_slot, x_blocks, zinv_blocks):
    row_count = lax.axis_size("row")
    col_count = lax.axis_size("col")
    groups, order, width = basis.shape
    owned = x_blocks.shape[0]
    places = GMAX // col_count
    capacity = (groups + row_count - 1) // row_count
    half = groups // 2
    note_rows = round_up(groups, 16)
    sizes = (groups, places, width, half, note_rows)

    ring = ring_order(col_count)
    place_of = {col: k for k, col in enumerate(ring)}
    ahead = [(ring[k], ring[(k + 1) % col_count]) for k in range(col_count)]
    behind = [(there, here) for here, there in ahead]
    full_steps = (col_count - 1) // 2
    split = col_count % 2 == 0 and col_count > 1

    x_parts, z_parts = [x_blocks], [zinv_blocks]
    x_from, z_from = [0], [0]
    going = [[x_blocks, zinv_blocks], [x_blocks, zinv_blocks]]
    for step in range(1, full_steps + 1):
        for way, (pairs, sign) in enumerate(((ahead, -1), (behind, 1))):
            going[way] = [lax.ppermute(held, "col", pairs) for held in going[way]]
            x_parts.append(going[way][0])
            z_parts.append(going[way][1])
            x_from.append(sign * step)
            z_from.append(sign * step)
    if split:
        x_parts.append(lax.ppermute(going[0][0], "col", ahead))
        z_parts.append(lax.ppermute(going[1][1], "col", behind))
        x_from.append(-(full_steps + 1))
        z_from.append(full_steps + 1)

    def table(offsets):
        return [
            [ring[(place_of[col] + offset) % col_count] for offset in offsets]
            for col in range(col_count)
        ]

    bins = pack(group_slot, row_index, basis, row_count, capacity, owned)
    got = [bins[0]]
    for shift in range(1, row_count):
        pairs = [(k, (k + shift) % row_count) for k in range(row_count)]
        got.append(lax.ppermute(bins[shift], "row", pairs))
    own = compact(got, capacity, groups, width, half, note_rows)

    own, x_parts, z_parts = lax.optimization_barrier((own, x_parts, z_parts))
    *weights, out = first_tiles(x_parts, z_parts, own, (table(x_from), table(z_from)), sizes)

    middle = half * width
    both = [(0, half, 0), (half, groups - half, middle + note_rows)]
    going = [own, own]
    for step in range(1, full_steps + 1):
        arrived = [lax.ppermute(going[0], "col", ahead), lax.ppermute(going[1], "col", behind)]
        going, out = lax.optimization_barrier((arrived, out))
        plans = [(middle, both, True)] * 2
        out = next_tiles(going, plans, weights, out, sizes)
    if split:
        lower = lax.ppermute(going[0][: middle + note_rows], "col", ahead)
        upper = lax.ppermute(going[1][middle:], "col", behind)
        plans = [(middle, [(0, half, 0)], True), (0, [(half, groups - half, note_rows)], False)]
        out = next_tiles([lower, upper], plans, weights, out, sizes)
    return out


def solution(mesh):
    placed = (
        P(("row", "col"), None, None),
        P(("row", "col"), None),
        P(("row", "col")),
        P("row", "col", None),
        P("row", "col", None),
    )
    return jax.shard_map(
        body, mesh=mesh, in_specs=placed, out_specs=P("row", None, "col"), check_vma=False
    )
```

time: 471 us -> 151 us (0.32)
  waiting for transfers between devices: 186 us -> 47.5 us
  matrix products: 102 us -> 0 us
  Pallas kernels: 0 us -> 74.7 us
  local copies, waits for them, and re-layouts: 64.7 us -> 2.72 us
  blocking collectives: 52.8 us -> 0 us
  other arithmetic: 39 us -> 0 us
  starting transfers between devices: 11.1 us -> 25.3 us
  between operations: 13.2 us -> 0.28 us
    all_gather x3 -> x0, waiting for transfers between devices: 169 us -> none  [the longest x1 134 us: body(): lax.all_gather(near_basis, 'col', axis=1, tiled=True)]
    dot_general x55 -> x0, matrix products: 102 us -> none  [the longest x12 22.9 us: pair_tiles(): jnp.einsum('pcn,snk->pcsk', images, near_basis, preferred_element_type=jn...]
    pallas_call x0 -> x7, Pallas kernels: none -> 74.7 us  [the longest x4 59.9 us: next_tiles(): pl.pallas_call(functools.partial(next_kernel, (groups, places, width, not...]
    all_gather x2 -> x0, blocking collectives: 52.8 us -> none  [the longest x1 31.7 us: body(): lax.all_gather(near_rows, 'col', axis=1, tiled=True)]
    ppermute x0 -> x25, waiting for transfers between devices: none -> 47.5 us  [the longest x3 16.5 us: body(): lax.ppermute(going[0], 'col', ahead)]
    ppermute x0 -> x25, starting transfers between devices: none -> 25.3 us  [the longest x12 13.5 us: body(): going[way] = [lax.ppermute(held, 'col', pairs) for held in going[way]]]
    squeeze x24 -> x0, local copies, waits for them, and re-layouts: 23.4 us -> none  [the longest x12 20.8 us: body(): lax.map(pair_tiles, (stacked, x_full, z_full, rows_all, mask_all, near_ba...]
    mul x12 -> x0, other arithmetic: 22.2 us -> none  [pair_tiles(): tile_sum = tile_sum * row_mask[:, None, None] * column_mask[None, None, :]]
  transfers between devices with their start and end apart: 6 -> 25, of which waited for: 3 -> 12; matrix products, arithmetic and copies ran while one was open for 5% -> 0% of each run, Pallas kernels for 0% -> 43%
where the time goes in v1:
time: 151 us
  Pallas kernels  74.7 us (49%)
  waiting for transfers between devices  47.5 us (31%)
  starting transfers between devices  25.3 us (17%)
  local copies, waits for them, and re-layouts  2.72 us (2%)
    pallas_call x4, Pallas kernels, next_tiles(): pl.pallas_call(functools.partial(next_kernel, (groups, places, width, not...  59.9 us
    ppermute x3, waiting for transfers between devices, body(): lax.ppermute(going[0], 'col', ahead)  16.5 us
    ppermute x3, waiting for transfers between devices, body(): lax.ppermute(going[1], 'col', behind)  14.5 us
    ppermute x12, starting transfers between devices, body(): going[way] = [lax.ppermute(held, 'col', pairs) for held in going[way]]  13.5 us
    ppermute x12, waiting for transfers between devices, body(): going[way] = [lax.ppermute(held, 'col', pairs) for held in going[way]]  13.5 us
    pallas_call x1, Pallas kernels, first_tiles(): pl.pallas_call(functools.partial(first_kernel, (groups, places, width, ha...  11.1 us
    ppermute x3, starting transfers between devices, body(): lax.ppermute(going[1], 'col', behind)  3.89 us
  transfers between devices with their start and end apart: 25, of which 12 were waited for; matrix products, arithmetic and copies ran while one was open for 0% of the time, Pallas kernels for 43%

profile of v1, /device:TPU:0, one launch (start us, length us, event | category | flops | bytes accessed | tf_op | source)
XLA Modules:
  0.0 150.6 jit_solution(12567293182649309296)
XLA Ops:
  0.0 3.0 %collective-permute-start.3 = (bf16[12,32,256]{2,1,0:T(8,128)(2,1)}, bf16[12,32,256]{2,1,0:T(8,128)(2,1)S(1)}, u32[]{:S(2)}, u32[]{:S(2)}) collective-permute-start(bf16[12,32,256]{2,1,0:T(8,128)(2,1)} %refs_0_), channel_id=1, source_target_pairs={{1,3},{3,5},{5,7},{7,6},{6,4},{4,2},{2,0},{0,1},{9,11},{11,13},{13... | collective-permute-start | bytes 589832 | tf_op jit(solution)/shard_map/ppermute | solution.py:454
  3.0 2.0 %collective-permute-start.11 = (bf16[12,32,256]{2,1,0:T(8,128)(2,1)}, bf16[12,32,256]{2,1,0:T(8,128)(2,1)S(1)}, u32[]{:S(2)}, u32[]{:S(2)}) collective-permute-start(bf16[12,32,256]{2,1,0:T(8,128)(2,1)} %refs_8_), channel_id=1, source_target_pairs={{3,1},{5,3},{7,5},{6,7},{4,6},{2,4},{0,2},{1,0},{11,9},{13,11},{15... | collective-permute-start | bytes 589832 | tf_op jit(solution)/shard_map/ppermute | solution.py:454
  5.1 1.3 copy-done
  6.3 0.7 copy-done.1
  7.7 2.3 %pack.1 = (bf16[656,256]{1,0:T(8,128)(2,1)S(1)}, bf16[656,256]{1,0:T(8,128)(2,1)S(1)}, bf16[656,256]{1,0:T(8,128)(2,1)S(1)}, bf16[656,256]{1,0:T(8,128)(2,1)S(1)}) custom-call(s32[18]{0:T(128)S(1)} %copy-done.2, s32[18,128]{1,0:T(8,128)S(1)} %copy-done.1, bf16[18,256,128]{2,1,0:T(8,128)(2,1)S(1)} %copy-done), custom_call_target="tpu_custom_call" | custom-call | tf_op jit(solution)/shard_map/pack/pallas_call | solution.py:87
  10.1 1.6 %collective-permute-start.1 = (bf16[656,256]{1,0:T(8,128)(2,1)S(1)}, bf16[656,256]{1,0:T(8,128)(2,1)S(1)}, u32[]{:S(2)}, u32[]{:S(2)}) collective-permute-start(bf16[656,256]{1,0:T(8,128)(2,1)S(1)} %get-tuple-element.42), channel_id=1, source_target_pairs={{0,16},{8,24},{16,0},{24,8},{1,17},{9,25},{17,1},{25,9},{2,18},{10... | collective-permute-start | bytes 1007624 | tf_op jit(solution)/shard_map/ppermute | solution.py:475
  12.1 1.5 %collective-permute-start.5 = (bf16[12,32,256]{2,1,0:T(8,128)(2,1)S(1)}, bf16[12,32,256]{2,1,0:T(8,128)(2,1)S(1)}, u32[]{:S(2)}, u32[]{:S(2)}) collective-permute-start(bf16[12,32,256]{2,1,0:T(8,128)(2,1)S(1)} %collective-permute-done.3.refs_1_), channel_id=1, source_target_pairs={{1,3},{3,5},{5,7},{7,6},{6,4},{4,2},{2,0},{0,1},{9,11},{11,13},{13... | collective-permute-start | bytes 589832 | tf_op jit(solution)/shard_map/ppermute | solution.py:454
  14.1 5.5 %collective-permute-done.10.refs_9_ = bf16[12,32,256]{2,1,0:T(8,128)(2,1)S(1)} collective-permute-done((bf16[12,32,256]{2,1,0:T(8,128)(2,1)}, bf16[12,32,256]{2,1,0:T(8,128)(2,1)S(1)}, u32[]{:S(2)}, u32[]{:S(2)}) %collective-permute-start.10) | collective-permute-done | bytes 196640 | tf_op jit(solution)/shard_map/ppermute | solution.py:454
  19.6 1.6 %collective-permute-start.6 = (bf16[12,32,256]{2,1,0:T(8,128)(2,1)S(1)}, bf16[12,32,256]{2,1,0:T(8,128)(2,1)S(1)}, u32[]{:S(2)}, u32[]{:S(2)}) collective-permute-start(bf16[12,32,256]{2,1,0:T(8,128)(2,1)S(1)} %collective-permute-done.4.refs_2_), channel_id=1, source_target_pairs={{3,1},{5,3},{7,5},{6,7},{4,6},{2,4},{0,2},{1,0},{11,9},{13,11},{15... | collective-permute-start | bytes 589832 | tf_op jit(solution)/shard_map/ppermute | solution.py:454
  21.6 2.2 %collective-permute-done.5.refs_3_ = bf16[12,32,256]{2,1,0:T(8,128)(2,1)S(1)} collective-permute-done((bf16[12,32,256]{2,1,0:T(8,128)(2,1)S(1)}, bf16[12,32,256]{2,1,0:T(8,128)(2,1)S(1)}, u32[]{:S(2)}, u32[]{:S(2)}) %collective-permute-start.5) | collective-permute-done | bytes 196640 | tf_op jit(solution)/shard_map/ppermute | solution.py:454
  24.1 1.8 %collective-permute-start.15 = (bf16[12,32,256]{2,1,0:T(8,128)(2,1)S(1)}, bf16[12,32,256]{2,1,0:T(8,128)(2,1)S(1)}, u32[]{:S(2)}, u32[]{:S(2)}) collective-permute-start(bf16[12,32,256]{2,1,0:T(8,128)(2,1)S(1)} %collective-permute-done.13.refs_12_), channel_id=1, source_target_pairs={{3,1},{5,3},{7,5},{6,7},{4,6},{2,4},{0,2},{1,0},{11,9},{13,11},{15... | collective-permute-start | bytes 589832 | tf_op jit(solution)/shard_map/ppermute | solution.py:454
  25.9 1.6 %collective-permute-start.8 = (bf16[12,32,256]{2,1,0:T(8,128)(2,1)S(1)}, bf16[12,32,256]{2,1,0:T(8,128)(2,1)S(1)}, u32[]{:S(2)}, u32[]{:S(2)}) collective-permute-start(bf16[12,32,256]{2,1,0:T(8,128)(2,1)S(1)} %collective-permute-done.6.refs_4_), channel_id=1, source_target_pairs={{3,1},{5,3},{7,5},{6,7},{4,6},{2,4},{0,2},{1,0},{11,9},{13,11},{15... | collective-permute-start | bytes 589832 | tf_op jit(solution)/shard_map/ppermute | solution.py:454
  27.5 1.5 %collective-permute-done.12.refs_11_ = bf16[12,32,256]{2,1,0:T(8,128)(2,1)S(1)} collective-permute-done((bf16[12,32,256]{2,1,0:T(8,128)(2,1)S(1)}, bf16[12,32,256]{2,1,0:T(8,128)(2,1)S(1)}, u32[]{:S(2)}, u32[]{:S(2)}) %collective-permute-start.12) | collective-permute-done | bytes 196640 | tf_op jit(solution)/shard_map/ppermute | solution.py:454
  29.5 3.4 %collective-permute-done.7.refs_5_ = bf16[12,32,256]{2,1,0:T(8,128)(2,1)S(1)} collective-permute-done((bf16[12,32,256]{2,1,0:T(8,128)(2,1)S(1)}, bf16[12,32,256]{2,1,0:T(8,128)(2,1)S(1)}, u32[]{:S(2)}, u32[]{:S(2)}) %collective-permute-start.7) | collective-permute-done | bytes 196640 | tf_op jit(solution)/shard_map/ppermute | solution.py:454
  33.0 1.9 %collective-permute-start.16 = (bf16[12,32,256]{2,1,0:T(8,128)(2,1)S(1)}, bf16[12,32,256]{2,1,0:T(8,128)(2,1)S(1)}, u32[]{:S(2)}, u32[]{:S(2)}) collective-permute-start(bf16[12,32,256]{2,1,0:T(8,128)(2,1)S(1)} %collective-permute-done.15.refs_14_), channel_id=1, source_target_pairs={{3,1},{5,3},{7,5},{6,7},{4,6},{2,4},{0,2},{1,0},{11,9},{13,11},{15... | collective-permute-start | bytes 589832 | tf_op jit(solution)/shard_map/ppermute | solution.py:461
  34.9 1.4 compact.1.refs_16_
  36.3 0.8 collective-permute-done.14.refs_13_
  37.1 2.9 %collective-permute-done.9.refs_7_ = bf16[12,32,256]{2,1,0:T(8,128)(2,1)S(1)} collective-permute-done((bf16[12,32,256]{2,1,0:T(8,128)(2,1)S(1)}, bf16[12,32,256]{2,1,0:T(8,128)(2,1)S(1)}, u32[]{:S(2)}, u32[]{:S(2)}) %collective-permute-start.9) | collective-permute-done | bytes 196640 | tf_op jit(solution)/shard_map/ppermute | solution.py:460
  40.0 1.6 %collective-permute-start.18 = (bf16[2336,256]{1,0:T(8,128)(2,1)S(1)}, bf16[2336,256]{1,0:T(8,128)(2,1)S(1)}, u32[]{:S(2)}, u32[]{:S(2)}) collective-permute-start(bf16[2336,256]{1,0:T(8,128)(2,1)S(1)} %compact.1.refs_16_), channel_id=1, source_target_pairs={{3,1},{5,3},{7,5},{6,7},{4,6},{2,4},{0,2},{1,0},{11,9},{13,11},{15... | collective-permute-start | bytes 3588104 | tf_op jit(solution)/shard_map/ppermute | solution.py:485
  42.1 11.1 %first_tiles.1 = (bf16[12,256,256]{2,1,0:T(8,128)(2,1)S(1)}, bf16[12,256,256]{2,1,0:T(8,128)(2,1)S(1)}, bf16[12,256,256]{2,1,0:T(8,128)(2,1)S(1)}, bf16[12,256,256]{2,1,0:T(8,128)(2,1)S(1)}, f32[12,2048,256]{2,1,0:T(8,128)}) custom-call(bf16[12,32,256]{2,1,0:T(8,128)(2,1)S(1)} %copy-done.3, bf16[12,32,256]{2,1,0:T(8,128)(2,1)S(1)} %collective-permute-done.3.refs_1_, ...), custom_call_target="tpu_custom_call" | custom-call | flops 3623878656 | bytes 3538944 | tf_op jit(solution)/shard_map/first_tiles/pallas_call | solution.py:354
  53.2 13.9 %collective-permute-done.18.refs_1_ = bf16[2336,256]{1,0:T(8,128)(2,1)S(1)} collective-permute-done((bf16[2336,256]{1,0:T(8,128)(2,1)S(1)}, bf16[2336,256]{1,0:T(8,128)(2,1)S(1)}, u32[]{:S(2)}, u32[]{:S(2)}) %collective-permute-start.18) | collective-permute-done | bytes 1196064 | tf_op jit(solution)/shard_map/ppermute | solution.py:485
  67.1 1.3 collective-permute-done.17.refs_0_
  68.8 1.6 %collective-permute-start.20 = (bf16[2336,256]{1,0:T(8,128)(2,1)S(1)}, bf16[2336,256]{1,0:T(8,128)(2,1)S(1)}, u32[]{:S(2)}, u32[]{:S(2)}) collective-permute-start(bf16[2336,256]{1,0:T(8,128)(2,1)S(1)} %collective-permute-done.18.refs_1_), channel_id=1, source_target_pairs={{3,1},{5,3},{7,5},{6,7},{4,6},{2,4},{0,2},{1,0},{11,9},{13,11},{15... | collective-permute-start | bytes 3588104 | tf_op jit(solution)/shard_map/ppermute | solution.py:485
  70.4 16.7 %next_tiles.4.refs_6_ = f32[12,2048,256]{2,1,0:T(8,128)} custom-call(bf16[2336,256]{1,0:T(8,128)(2,1)S(1)} %collective-permute-done.17.refs_0_, bf16[2336,256]{1,0:T(8,128)(2,1)S(1)} %collective-permute-done.18.refs_1_, bf16[12,256,256]{2,1,0:T(8,128)(2,1)S(1)} %get-tuple-element.64.refs_2_, ...), custom_call_target="tpu_custom_call", output_to_operand_aliasing={{}: (6, {})} | custom-call | flops 7247757312 | bytes 7077888 | tf_op jit(solution)/shard_map/next_tiles/pallas_call | solution.py:406
  87.1 7.9 %collective-permute-done.19.refs_0_ = bf16[2336,256]{1,0:T(8,128)(2,1)S(1)} collective-permute-done((bf16[2336,256]{1,0:T(8,128)(2,1)S(1)}, bf16[2336,256]{1,0:T(8,128)(2,1)S(1)}, u32[]{:S(2)}, u32[]{:S(2)}) %collective-permute-start.19) | collective-permute-done | bytes 1196064 | tf_op jit(solution)/shard_map/ppermute | solution.py:485
  94.9 1.3 collective-permute-start.21
  96.2 0.7 collective-permute-start.22
  97.0 16.6 %next_tiles.5.refs_6_ = f32[12,2048,256]{2,1,0:T(8,128)} custom-call(bf16[2336,256]{1,0:T(8,128)(2,1)S(1)} %collective-permute-done.19.refs_0_, bf16[2336,256]{1,0:T(8,128)(2,1)S(1)} %collective-permute-done.20.refs_1_, bf16[12,256,256]{2,1,0:T(8,128)(2,1)S(1)} %get-tuple-element.64.refs_2_, ...), custom_call_target="tpu_custom_call", output_to_operand_aliasing={{}: (6, {})} | custom-call | flops 7247757312 | bytes 7077888 | tf_op jit(solution)/shard_map/next_tiles/pallas_call | solution.py:406
  113.6 7.4 %collective-permute-done.21.refs_0_ = bf16[2336,256]{1,0:T(8,128)(2,1)S(1)} collective-permute-done((bf16[2336,256]{1,0:T(8,128)(2,1)S(1)}, bf16[2336,256]{1,0:T(8,128)(2,1)S(1)}, u32[]{:S(2)}, u32[]{:S(2)}) %collective-permute-start.21) | collective-permute-done | bytes 1196064 | tf_op jit(solution)/shard_map/ppermute | solution.py:485
  121.7 1.4 collective-permute-start.23
  123.8 16.7 %next_tiles.6.refs_6_ = f32[12,2048,256]{2,1,0:T(8,128)} custom-call(bf16[2336,256]{1,0:T(8,128)(2,1)S(1)} %collective-permute-done.21.refs_0_, bf16[2336,256]{1,0:T(8,128)(2,1)S(1)} %collective-permute-done.22.refs_1_, bf16[12,256,256]{2,1,0:T(8,128)(2,1)S(1)} %get-tuple-element.64.refs_2_, ...), custom_call_target="tpu_custom_call", output_to_operand_aliasing={{}: (6, {})} | custom-call | flops 7247757312 | bytes 7077888 | tf_op jit(solution)/shard_map/next_tiles/pallas_call | solution.py:406
  140.5 9.9 %next_tiles.7 = f32[12,2048,256]{2,1,0:T(8,128)} custom-call(bf16[1184,256]{1,0:T(8,128)(2,1)S(1)} %collective-permute-done.23.refs_0_, bf16[1184,256]{1,0:T(8,128)(2,1)S(1)} %collective-permute-done.24.refs_1_, bf16[12,256,256]{2,1,0:T(8,128)(2,1)S(1)} %get-tuple-element.64.refs_2_, ...), custom_call_target="tpu_custom_call", output_to_operand_aliasing={{}: (6, {})} | custom-call | flops 3623878656 | bytes 3538944 | tf_op jit(solution)/shard_map/next_tiles/pallas_call | solution.py:406
  (37 shorter events, 5.3 us)
Async XLA Ops:
  0.0 11.7 %collective-permute-start.3 = (bf16[12,32,256]{2,1,0:T(8,128)(2,1)}, bf16[12,32,256]{2,1,0:T(8,128)(2,1)S(1)}, u32[]{:S(2)}, u32[]{:S(2)}) collective-permute-start(bf16[12,32,256]{2,1,0:T(8,128)(2,1)} %refs_0_), channel_id=1, source_target_pairs={{1,3},{3,5},{5,7},{7,6},{6,4},{4,2},{2,0},{0,1},{9,11},{11,13},{13... | collective-permute-start | bytes 589832 | tf_op jit(solution)/shard_map/ppermute | solution.py:454
  3.0 9.1 %collective-permute-start.4 = (bf16[12,32,256]{2,1,0:T(8,128)(2,1)}, bf16[12,32,256]{2,1,0:T(8,128)(2,1)S(1)}, u32[]{:S(2)}, u32[]{:S(2)}) collective-permute-start(bf16[12,32,256]{2,1,0:T(8,128)(2,1)} %refs_0_), channel_id=1, source_target_pairs={{3,1},{5,3},{7,5},{6,7},{4,6},{2,4},{0,2},{1,0},{11,9},{13,11},{15... | collective-permute-start | bytes 589832 | tf_op jit(solution)/shard_map/ppermute | solution.py:454
  3.0 10.7 %collective-permute-start.11 = (bf16[12,32,256]{2,1,0:T(8,128)(2,1)}, bf16[12,32,256]{2,1,0:T(8,128)(2,1)S(1)}, u32[]{:S(2)}, u32[]{:S(2)}) collective-permute-start(bf16[12,32,256]{2,1,0:T(8,128)(2,1)} %refs_8_), channel_id=1, source_target_pairs={{3,1},{5,3},{7,5},{6,7},{4,6},{2,4},{0,2},{1,0},{11,9},{13,11},{15... | collective-permute-start | bytes 589832 | tf_op jit(solution)/shard_map/ppermute | solution.py:454
  5.1 1.3 copy-start
  6.3 0.7 copy-start.1
  7.0 0.7 copy-start.2
  7.7 34.4 %copy-start.3 = (bf16[12,32,256]{2,1,0:T(8,128)(2,1)S(1)}, bf16[12,32,256]{2,1,0:T(8,128)(2,1)}, u32[]{:S(2)}) copy-start(bf16[12,32,256]{2,1,0:T(8,128)(2,1)} %refs_0_) | copy-start | bytes 589828
  7.7 34.4 %copy-start.4 = (bf16[12,32,256]{2,1,0:T(8,128)(2,1)S(1)}, bf16[12,32,256]{2,1,0:T(8,128)(2,1)}, u32[]{:S(2)}) copy-start(bf16[12,32,256]{2,1,0:T(8,128)(2,1)} %refs_8_) | copy-start | bytes 589828
  10.0 11.1 %collective-permute-start = (bf16[656,256]{1,0:T(8,128)(2,1)S(1)}, bf16[656,256]{1,0:T(8,128)(2,1)S(1)}, u32[]{:S(2)}, u32[]{:S(2)}) collective-permute-start(bf16[656,256]{1,0:T(8,128)(2,1)S(1)} %get-tuple-element.41), channel_id=1, source_target_pairs={{0,8},{8,16},{16,24},{24,0},{1,9},{9,17},{17,25},{25,1},{2,10},{10... | collective-permute-start | bytes 1007624 | tf_op jit(solution)/shard_map/ppermute | solution.py:475
  10.1 15.7 %collective-permute-start.1 = (bf16[656,256]{1,0:T(8,128)(2,1)S(1)}, bf16[656,256]{1,0:T(8,128)(2,1)S(1)}, u32[]{:S(2)}, u32[]{:S(2)}) collective-permute-start(bf16[656,256]{1,0:T(8,128)(2,1)S(1)} %get-tuple-element.42), channel_id=1, source_target_pairs={{0,16},{8,24},{16,0},{24,8},{1,17},{9,25},{17,1},{25,9},{2,18},{10... | collective-permute-start | bytes 1007624 | tf_op jit(solution)/shard_map/ppermute | solution.py:475
  11.7 7.9 %collective-permute-start.10 = (bf16[12,32,256]{2,1,0:T(8,128)(2,1)}, bf16[12,32,256]{2,1,0:T(8,128)(2,1)S(1)}, u32[]{:S(2)}, u32[]{:S(2)}) collective-permute-start(bf16[12,32,256]{2,1,0:T(8,128)(2,1)} %refs_8_), channel_id=1, source_target_pairs={{1,3},{3,5},{5,7},{7,6},{6,4},{4,2},{2,0},{0,1},{9,11},{11,13},{13... | collective-permute-start | bytes 589832 | tf_op jit(solution)/shard_map/ppermute | solution.py:454
  12.1 11.7 %collective-permute-start.5 = (bf16[12,32,256]{2,1,0:T(8,128)(2,1)S(1)}, bf16[12,32,256]{2,1,0:T(8,128)(2,1)S(1)}, u32[]{:S(2)}, u32[]{:S(2)}) collective-permute-start(bf16[12,32,256]{2,1,0:T(8,128)(2,1)S(1)} %collective-permute-done.3.refs_1_), channel_id=1, source_target_pairs={{1,3},{3,5},{5,7},{7,6},{6,4},{4,2},{2,0},{0,1},{9,11},{11,13},{13... | collective-permute-start | bytes 589832 | tf_op jit(solution)/shard_map/ppermute | solution.py:454
  13.8 10.3 %collective-permute-start.13 = (bf16[12,32,256]{2,1,0:T(8,128)(2,1)S(1)}, bf16[12,32,256]{2,1,0:T(8,128)(2,1)S(1)}, u32[]{:S(2)}, u32[]{:S(2)}) collective-permute-start(bf16[12,32,256]{2,1,0:T(8,128)(2,1)S(1)} %collective-permute-done.11.refs_10_), channel_id=1, source_target_pairs={{3,1},{5,3},{7,5},{6,7},{4,6},{2,4},{0,2},{1,0},{11,9},{13,11},{15... | collective-permute-start | bytes 589832 | tf_op jit(solution)/shard_map/ppermute | solution.py:454
  19.6 6.3 %collective-permute-start.6 = (bf16[12,32,256]{2,1,0:T(8,128)(2,1)S(1)}, bf16[12,32,256]{2,1,0:T(8,128)(2,1)S(1)}, u32[]{:S(2)}, u32[]{:S(2)}) collective-permute-start(bf16[12,32,256]{2,1,0:T(8,128)(2,1)S(1)} %collective-permute-done.4.refs_2_), channel_id=1, source_target_pairs={{3,1},{5,3},{7,5},{6,7},{4,6},{2,4},{0,2},{1,0},{11,9},{13,11},{15... | collective-permute-start | bytes 589832 | tf_op jit(solution)/shard_map/ppermute | solution.py:454
  21.2 7.8 %collective-permute-start.12 = (bf16[12,32,256]{2,1,0:T(8,128)(2,1)S(1)}, bf16[12,32,256]{2,1,0:T(8,128)(2,1)S(1)}, u32[]{:S(2)}, u32[]{:S(2)}) collective-permute-start(bf16[12,32,256]{2,1,0:T(8,128)(2,1)S(1)} %collective-permute-done.10.refs_9_), channel_id=1, source_target_pairs={{1,3},{3,5},{5,7},{7,6},{6,4},{4,2},{2,0},{0,1},{9,11},{11,13},{13... | collective-permute-start | bytes 589832 | tf_op jit(solution)/shard_map/ppermute | solution.py:454
  23.8 9.1 %collective-permute-start.7 = (bf16[12,32,256]{2,1,0:T(8,128)(2,1)S(1)}, bf16[12,32,256]{2,1,0:T(8,128)(2,1)S(1)}, u32[]{:S(2)}, u32[]{:S(2)}) collective-permute-start(bf16[12,32,256]{2,1,0:T(8,128)(2,1)S(1)} %collective-permute-done.5.refs_3_), channel_id=1, source_target_pairs={{1,3},{3,5},{5,7},{7,6},{6,4},{4,2},{2,0},{0,1},{9,11},{11,13},{13... | collective-permute-start | bytes 589832 | tf_op jit(solution)/shard_map/ppermute | solution.py:454
  24.1 9.0 %collective-permute-start.15 = (bf16[12,32,256]{2,1,0:T(8,128)(2,1)S(1)}, bf16[12,32,256]{2,1,0:T(8,128)(2,1)S(1)}, u32[]{:S(2)}, u32[]{:S(2)}) collective-permute-start(bf16[12,32,256]{2,1,0:T(8,128)(2,1)S(1)} %collective-permute-done.13.refs_12_), channel_id=1, source_target_pairs={{3,1},{5,3},{7,5},{6,7},{4,6},{2,4},{0,2},{1,0},{11,9},{13,11},{15... | collective-permute-start | bytes 589832 | tf_op jit(solution)/shard_map/ppermute | solution.py:454
  25.8 9.1 %collective-permute-start.2 = (bf16[656,256]{1,0:T(8,128)(2,1)S(1)}, bf16[656,256]{1,0:T(8,128)(2,1)S(1)}, u32[]{:S(2)}, u32[]{:S(2)}) collective-permute-start(bf16[656,256]{1,0:T(8,128)(2,1)S(1)} %get-tuple-element.43), channel_id=1, source_target_pairs={{0,24},{8,0},{16,8},{24,16},{1,25},{9,1},{17,9},{25,17},{2,26},{10... | collective-permute-start | bytes 1007624 | tf_op jit(solution)/shard_map/ppermute | solution.py:475
  25.9 10.5 %collective-permute-start.8 = (bf16[12,32,256]{2,1,0:T(8,128)(2,1)S(1)}, bf16[12,32,256]{2,1,0:T(8,128)(2,1)S(1)}, u32[]{:S(2)}, u32[]{:S(2)}) collective-permute-start(bf16[12,32,256]{2,1,0:T(8,128)(2,1)S(1)} %collective-permute-done.6.refs_4_), channel_id=1, source_target_pairs={{3,1},{5,3},{7,5},{6,7},{4,6},{2,4},{0,2},{1,0},{11,9},{13,11},{15... | collective-permute-start | bytes 589832 | tf_op jit(solution)/shard_map/ppermute | solution.py:454
  29.0 8.1 %collective-permute-start.14 = (bf16[12,32,256]{2,1,0:T(8,128)(2,1)S(1)}, bf16[12,32,256]{2,1,0:T(8,128)(2,1)S(1)}, u32[]{:S(2)}, u32[]{:S(2)}) collective-permute-start(bf16[12,32,256]{2,1,0:T(8,128)(2,1)S(1)} %collective-permute-done.12.refs_11_), channel_id=1, source_target_pairs={{1,3},{3,5},{5,7},{7,6},{6,4},{4,2},{2,0},{0,1},{9,11},{11,13},{13... | collective-permute-start | bytes 589832 | tf_op jit(solution)/shard_map/ppermute | solution.py:454
  32.9 7.1 %collective-permute-start.9 = (bf16[12,32,256]{2,1,0:T(8,128)(2,1)S(1)}, bf16[12,32,256]{2,1,0:T(8,128)(2,1)S(1)}, u32[]{:S(2)}, u32[]{:S(2)}) collective-permute-start(bf16[12,32,256]{2,1,0:T(8,128)(2,1)S(1)} %collective-permute-done.7.refs_5_), channel_id=1, source_target_pairs={{1,3},{3,5},{5,7},{7,6},{6,4},{4,2},{2,0},{0,1},{9,11},{11,13},{13... | collective-permute-start | bytes 589832 | tf_op jit(solution)/shard_map/ppermute | solution.py:460
  33.0 7.0 %collective-permute-start.16 = (bf16[12,32,256]{2,1,0:T(8,128)(2,1)S(1)}, bf16[12,32,256]{2,1,0:T(8,128)(2,1)S(1)}, u32[]{:S(2)}, u32[]{:S(2)}) collective-permute-start(bf16[12,32,256]{2,1,0:T(8,128)(2,1)S(1)} %collective-permute-done.15.refs_14_), channel_id=1, source_target_pairs={{3,1},{5,3},{7,5},{6,7},{4,6},{2,4},{0,2},{1,0},{11,9},{13,11},{15... | collective-permute-start | bytes 589832 | tf_op jit(solution)/shard_map/ppermute | solution.py:461
  40.0 27.0 %collective-permute-start.18 = (bf16[2336,256]{1,0:T(8,128)(2,1)S(1)}, bf16[2336,256]{1,0:T(8,128)(2,1)S(1)}, u32[]{:S(2)}, u32[]{:S(2)}) collective-permute-start(bf16[2336,256]{1,0:T(8,128)(2,1)S(1)} %compact.1.refs_16_), channel_id=1, source_target_pairs={{3,1},{5,3},{7,5},{6,7},{4,6},{2,4},{0,2},{1,0},{11,9},{13,11},{15... | collective-permute-start | bytes 3588104 | tf_op jit(solution)/shard_map/ppermute | solution.py:485
  41.6 26.8 %collective-permute-start.17 = (bf16[2336,256]{1,0:T(8,128)(2,1)S(1)}, bf16[2336,256]{1,0:T(8,128)(2,1)S(1)}, u32[]{:S(2)}, u32[]{:S(2)}) collective-permute-start(bf16[2336,256]{1,0:T(8,128)(2,1)S(1)} %compact.1.refs_16_), channel_id=1, source_target_pairs={{1,3},{3,5},{5,7},{7,6},{6,4},{4,2},{2,0},{0,1},{9,11},{11,13},{13... | collective-permute-start | bytes 3588104 | tf_op jit(solution)/shard_map/ppermute | solution.py:485
  68.4 26.6 %collective-permute-start.19 = (bf16[2336,256]{1,0:T(8,128)(2,1)S(1)}, bf16[2336,256]{1,0:T(8,128)(2,1)S(1)}, u32[]{:S(2)}, u32[]{:S(2)}) collective-permute-start(bf16[2336,256]{1,0:T(8,128)(2,1)S(1)} %collective-permute-done.17.refs_0_), channel_id=1, source_target_pairs={{1,3},{3,5},{5,7},{7,6},{6,4},{4,2},{2,0},{0,1},{9,11},{11,13},{13... | collective-permute-start | bytes 3588104 | tf_op jit(solution)/shard_map/ppermute | solution.py:485
  68.8 26.1 %collective-permute-start.20 = (bf16[2336,256]{1,0:T(8,128)(2,1)S(1)}, bf16[2336,256]{1,0:T(8,128)(2,1)S(1)}, u32[]{:S(2)}, u32[]{:S(2)}) collective-permute-start(bf16[2336,256]{1,0:T(8,128)(2,1)S(1)} %collective-permute-done.18.refs_1_), channel_id=1, source_target_pairs={{3,1},{5,3},{7,5},{6,7},{4,6},{2,4},{0,2},{1,0},{11,9},{13,11},{15... | collective-permute-start | bytes 3588104 | tf_op jit(solution)/shard_map/ppermute | solution.py:485
  94.9 26.1 %collective-permute-start.21 = (bf16[2336,256]{1,0:T(8,128)(2,1)S(1)}, bf16[2336,256]{1,0:T(8,128)(2,1)S(1)}, u32[]{:S(2)}, u32[]{:S(2)}) collective-permute-start(bf16[2336,256]{1,0:T(8,128)(2,1)S(1)} %collective-permute-done.19.refs_0_), channel_id=1, source_target_pairs={{1,3},{3,5},{5,7},{7,6},{6,4},{4,2},{2,0},{0,1},{9,11},{11,13},{13... | collective-permute-start | bytes 3588104 | tf_op jit(solution)/shard_map/ppermute | solution.py:485
  96.2 25.4 %collective-permute-start.22 = (bf16[2336,256]{1,0:T(8,128)(2,1)S(1)}, bf16[2336,256]{1,0:T(8,128)(2,1)S(1)}, u32[]{:S(2)}, u32[]{:S(2)}) collective-permute-start(bf16[2336,256]{1,0:T(8,128)(2,1)S(1)} %collective-permute-done.20.refs_1_), channel_id=1, source_target_pairs={{3,1},{5,3},{7,5},{6,7},{4,6},{2,4},{0,2},{1,0},{11,9},{13,11},{15... | collective-permute-start | bytes 3588104 | tf_op jit(solution)/shard_map/ppermute | solution.py:485
  121.7 18.7 %collective-permute-start.23 = (bf16[1184,256]{1,0:T(8,128)(2,1)S(1)}, bf16[1184,256]{1,0:T(8,128)(2,1)S(1)}, u32[]{:S(2)}, u32[]{:S(2)}) collective-permute-start(bf16[1184,256]{1,0:T(8,128)(2,1)S(1)} %slice.6), channel_id=1, source_target_pairs={{1,3},{3,5},{5,7},{7,6},{6,4},{4,2},{2,0},{0,1},{9,11},{11,13},{13... | collective-permute-start | bytes 1818632 | tf_op jit(solution)/shard_map/ppermute | solution.py:490
  123.1 17.4 %collective-permute-start.24 = (bf16[1184,256]{1,0:T(8,128)(2,1)S(1)}, bf16[1184,256]{1,0:T(8,128)(2,1)S(1)}, u32[]{:S(2)}, u32[]{:S(2)}) collective-permute-start(bf16[1184,256]{1,0:T(8,128)(2,1)S(1)} %slice.7), channel_id=1, source_target_pairs={{3,1},{5,3},{7,5},{6,7},{4,6},{2,4},{0,2},{1,0},{11,9},{13,11},{15... | collective-permute-start | bytes 1818632 | tf_op jit(solution)/shard_map/ppermute | solution.py:491

commit v2 on v1

v2 whole, which is shorter than its diff:
```python
import functools
import math

import jax
import jax.numpy as jnp
from jax import lax
from jax.experimental import pallas as pl
from jax.experimental.pallas import tpu as pltpu
from jax.sharding import PartitionSpec as P

GMAX = 16
LANES = 128
VMEM_LIMIT = 32 * 1024 * 1024
UNROLL = 5


def round_up(value, unit):
    return (value + unit - 1) // unit * unit


def ring_order(count):
    inner = max(d for d in range(1, math.isqrt(count) + 1) if count % d == 0)
    outer = count // inner
    path = []
    for line in range(outer):
        places = range(1, inner) if line % 2 == 0 else range(inner - 1, 0, -1)
        path += [line * inner + place for place in places]
    return path + [line * inner for line in range(outer - 1, -1, -1)]


def dot(left, right):
    return jnp.dot(left, right, preferred_element_type=jnp.float32)


def partner(place, turn, count):
    return place ^ turn if count & (count - 1) == 0 else (place + turn) % count


def side_by_side(counts):
    return max(k for k in range(1, UNROLL + 1) if all(count % k == 0 for count in counts))


def cost(groups, order, width, near, extra_bytes=0):
    steps = groups * width * order * (4 * order + 8 * near)
    moved = groups * width * (2 * order + 4 * near) + extra_bytes
    return pl.CostEstimate(flops=2 * steps, bytes_accessed=moved, transcendentals=0)


def whole(space=pltpu.VMEM):
    return pl.BlockSpec(memory_space=space)


def pack_kernel(dims, slot_ref, rows_ref, basis_ref, *refs):
    row_count, capacity, owned = dims
    outs = refs[:row_count]
    bins, notes, facts, counts, sems = refs[row_count:]
    groups, order, width = basis_ref.shape
    my_row = lax.axis_index("row")
    notes[...] = jnp.zeros_like(notes)
    facts[...] = jnp.zeros_like(facts)
    for shift in range(row_count):
        counts[shift] = 0
    lane = lax.broadcasted_iota(jnp.int32, (1, LANES), 1)

    def place(g, carry):
        slot = slot_ref[g]
        block = slot // GMAX
        owner = block // owned
        if row_count & (row_count - 1) == 0:
            shift = owner ^ my_row
        else:
            shift = lax.rem(owner - my_row + row_count, row_count)
        at = counts[shift]
        counts[shift] = at + 1
        start = pl.multiple_of(notes.shape[1] + at * width, 16)
        bins[shift, pl.ds(start, width), :] = basis_ref[g].T
        notes[shift, pl.ds(at, 1), :] = rows_ref[pl.ds(g, 1), :].astype(jnp.float32)
        fact = jnp.where(lane == 0, block - owner * owned + 1, 0)
        fact = jnp.where(lane == 1, slot - block * GMAX, fact)
        facts[shift, pl.ds(at, 1), :] = fact.astype(jnp.float32)
        return carry

    lax.fori_loop(0, groups, place, 0)
    copies = []
    for shift in range(row_count):
        bins[shift, : notes.shape[1], :width] = notes[shift].astype(jnp.bfloat16)
        bins[shift, : notes.shape[1], width : width + LANES] = facts[shift].astype(jnp.bfloat16)
        copies.append(pltpu.make_async_copy(bins.at[shift], outs[shift], sems.at[shift]))
        copies[-1].start()
    for copy in copies:
        copy.wait()


def pack(slots, rows, basis, row_count, capacity, owned):
    groups, order, width = basis.shape
    note_rows = round_up(capacity, 16)
    shape = (capacity * width + note_rows, order)
    return pl.pallas_call(
        functools.partial(pack_kernel, (row_count, capacity, owned)),
        out_shape=[jax.ShapeDtypeStruct(shape, jnp.bfloat16)] * row_count,
        in_specs=[whole(pltpu.SMEM), whole(), whole()],
        out_specs=[whole(pl.ANY)] * row_count,
        scratch_shapes=[
            pltpu.VMEM((row_count,) + shape, jnp.bfloat16),
            pltpu.VMEM((row_count, note_rows, width), jnp.float32),
            pltpu.VMEM((row_count, note_rows, LANES), jnp.float32),
            pltpu.SMEM((row_count,), jnp.int32),
            pltpu.SemaphoreType.DMA((row_count,)),
        ],
        compiler_params=pltpu.CompilerParams(vmem_limit_bytes=VMEM_LIMIT),
        name="pack",
    )(slots, rows, basis)


def compact_kernel(dims, *refs):
    capacity, width, skip, take, bin_notes, note_rows = dims
    bin_count = len(refs) - 9
    bins, out = refs[:bin_count], refs[bin_count]
    notes_in, notes, facts_in, facts, numbers, scalars, counts, sem = refs[bin_count + 1 :]
    for shift in range(bin_count):
        notes_in[shift] = bins[shift][:bin_notes, :width].astype(jnp.float32)
        facts_in[shift] = bins[shift][:bin_notes, width : width + LANES].astype(jnp.float32)
        numbers[shift] = facts_in[shift].astype(jnp.int32)
    copy = pltpu.make_async_copy(numbers, scalars, sem)
    copy.start()
    notes[...] = jnp.zeros_like(notes)
    facts[...] = jnp.zeros_like(facts)
    counts[0] = 0
    copy.wait()
    for shift in range(bin_count):
        for k in range(capacity):
            here = scalars[shift, k, 0] > 0
            seen = counts[0]
            counts[0] = seen + here.astype(jnp.int32)
            place = seen - skip

            @pl.when(here & (place >= 0) & (place < take))
            def _():
                notes[pl.ds(place, 1), :] = notes_in[shift, k : k + 1, :]
                facts[pl.ds(place, 1), :] = facts_in[shift, k : k + 1, :]
                start = pl.multiple_of(note_rows + place * width, 16)
                source = bin_notes + k * width
                out[pl.ds(start, width), :] = bins[shift][source : source + width, :]

    out[:note_rows, :width] = notes[...].astype(jnp.bfloat16)
    out[:note_rows, width : width + LANES] = facts[...].astype(jnp.bfloat16)


def compact(bins, capacity, width, skip, take, note_rows):
    bin_count = len(bins)
    order = bins[0].shape[1]
    bin_notes = bins[0].shape[0] - capacity * width
    dims = (capacity, width, skip, take, bin_notes, note_rows)
    return pl.pallas_call(
        functools.partial(compact_kernel, dims),
        out_shape=jax.ShapeDtypeStruct((note_rows + take * width, order), jnp.bfloat16),
        in_specs=[whole()] * bin_count,
        out_specs=whole(),
        scratch_shapes=[
            pltpu.VMEM((bin_count, bin_notes, width), jnp.float32),
            pltpu.VMEM((note_rows, width), jnp.float32),
            pltpu.VMEM((bin_count, bin_notes, LANES), jnp.float32),
            pltpu.VMEM((note_rows, LANES), jnp.float32),
            pltpu.VMEM((bin_count, bin_notes, LANES), jnp.int32),
            pltpu.SMEM((bin_count, bin_notes, LANES), jnp.int32),
            pltpu.SMEM((1,), jnp.int32),
            pltpu.SemaphoreType.DMA,
        ],
        compiler_params=pltpu.CompilerParams(vmem_limit_bytes=VMEM_LIMIT),
        name="compact",
    )(*bins)


def read_notes(pieces, notes, facts):
    note_rows = notes.shape[0] // len(pieces)
    width = notes.shape[1]
    for k, piece in enumerate(pieces):
        rows = slice(k * note_rows, (k + 1) * note_rows)
        notes[rows, :] = piece[:note_rows, :width].astype(jnp.float32)
        numbers = piece[:note_rows, width : width + LANES].astype(jnp.float32)
        facts[rows, :] = numbers.astype(jnp.int32)


def spot_of(facts, note):
    fact = facts[pl.ds(note, 1), :]
    return fact[0, 0] - 1, fact[0, 1]


def tiles_of(spans, width, notes, facts, weights, out, stage, stage_sems):
    x_ref, z_ref, near_ref, pick_ref = weights
    order = x_ref.shape[1]
    unroll = stage.shape[0] // 2
    lane = lax.broadcasted_iota(jnp.int32, (width, order), 1).astype(jnp.float32)
    repeats = order // width

    def send(b, p, slot):
        start = pl.multiple_of(p * width, width)
        return pltpu.make_async_copy(
            stage.at[slot], out.at[b, pl.ds(start, width), :], stage_sems.at[slot]
        )

    def images(piece, note, start):
        b, p = spot_of(facts, note)
        vectors = piece[pl.ds(start, width), :]
        turned = jnp.broadcast_to(notes[pl.ds(note, 1), :], (width, width)).T
        row_pick = (jnp.concatenate([turned] * repeats, axis=1) == lane).astype(jnp.bfloat16)
        left = jnp.concatenate([vectors, row_pick], axis=0)
        x_half = dot(left, x_ref[b]).astype(jnp.bfloat16)
        z_half = dot(left, z_ref[b]).astype(jnp.bfloat16)
        return b, p, jnp.concatenate([x_half, z_half], axis=0)

    def tile(b, p, halves, slot):
        su, se = dot(halves, near_ref[b]), dot(halves, pick_ref[b])
        su_yx, su_x, su_yz, su_z = (su[k * width : (k + 1) * width] for k in range(4))
        se_yx, se_x, se_yz, se_z = (se[k * width : (k + 1) * width] for k in range(4))
        stage[slot] = (su_x * se_yz + se_x * su_yz) + (su_yx * se_z + se_yx * su_z)
        send(b, p, slot).start()

    def side_by_side_tiles(piece, first, base, count, bank):
        found = [
            images(piece, first + k, pl.multiple_of(base + k * width, 16)) for k in range(count)
        ]
        for k, held in enumerate(found):
            tile(*held, bank * unroll + k)

    waiting = [0, 0]

    def drain(bank, count):
        for k in range(count):
            send(0, 0, bank * unroll + k).wait()

    rounds = 0
    for piece, base, first, count in spans:
        full, rest = divmod(count, unroll)
        if full > 2:
            for bank in range(2):
                drain(bank, waiting[bank])

            def body(i, carry, piece=piece, base=base, first=first):
                bank = lax.rem(i, 2)

                @pl.when(i >= 2)
                def _():
                    drain(bank, unroll)

                at = i * unroll
                side_by_side_tiles(piece, first + at, base + at * width, unroll, bank)
                return carry

            lax.fori_loop(0, full, body, 0)
            waiting[:] = [unroll, unroll]
            rounds = full
        sizes = [] if full > 2 else [unroll] * full
        done = full * unroll if full > 2 else 0
        for size in sizes + ([rest] if rest else []):
            bank = rounds % 2
            drain(bank, waiting[bank])
            side_by_side_tiles(piece, first + done, base + done * width, size, bank)
            waiting[bank] = size
            done += size
            rounds += 1
    for bank in range(2):
        drain(bank, waiting[bank])


def blank_kernel(blocks, *refs):
    out, blank, sems = refs[-3:]
    blank[...] = jnp.zeros_like(blank)
    deep_rows = blank.shape[0]
    per_block = out.shape[1] // deep_rows
    copies = []
    for b in blocks:
        for k in range(per_block):
            copies.append(
                pltpu.make_async_copy(
                    blank,
                    out.at[b, pl.ds(k * deep_rows, deep_rows), :],
                    sems.at[(b - blocks[0]) * per_block + k],
                )
            )
            copies[-1].start()
    for copy in copies:
        copy.wait()


def blank_tiles(shape, blocks, after, out=None):
    held = list(after) if out is None else [*after, out]
    deep_rows = shape[1] // 2
    return pl.pallas_call(
        functools.partial(blank_kernel, blocks),
        out_shape=jax.ShapeDtypeStruct(shape, jnp.float32),
        in_specs=[whole(pl.ANY)] * len(held),
        out_specs=whole(pl.ANY),
        input_output_aliases={} if out is None else {len(after): 0},
        scratch_shapes=[
            pltpu.VMEM((deep_rows, shape[2]), jnp.float32),
            pltpu.SemaphoreType.DMA((2 * len(blocks),)),
        ],
        cost_estimate=pl.CostEstimate(
            flops=0, bytes_accessed=4 * len(blocks) * shape[1] * shape[2], transcendentals=0
        ),
        compiler_params=pltpu.CompilerParams(vmem_limit_bytes=VMEM_LIMIT),
        name="blank_tiles",
    )(*held)


def settle_kernel(dims, *refs):
    counts, places, width, note_rows = dims
    pieces, (near_ref, pick_ref) = refs[:2], refs[2:4]
    notes, facts, near_rows = refs[4:]
    my_col = lax.axis_index("col")
    owned, order = near_ref.shape[:2]
    near_ref[...] = jnp.zeros_like(near_ref)
    near_rows[...] = jnp.full(near_rows.shape, -1.0, jnp.float32)
    read_notes(pieces, notes, facts)

    for piece, count, first in zip(pieces, counts, (0, note_rows)):

        def settle(g, carry, piece=piece, first=first):
            b, place = spot_of(facts, first + g)
            place = place - my_col * places
            start = pl.multiple_of(note_rows + g * width, 16)
            turned = piece[pl.ds(start, width), :].T
            for k in range(places):

                @pl.when(place == k)
                def _():
                    near_ref[b, :, k * width : (k + 1) * width] = turned
                    near_rows[b, k : k + 1, :] = notes[pl.ds(first + g, 1), :]

            return carry

        lax.fori_loop(0, count, settle, 0)
    deep = lax.broadcasted_iota(jnp.int32, (order, width), 0).astype(jnp.float32)

    def picks(b, carry):
        for k in range(places):
            hit = near_rows[b, k : k + 1, :] == deep
            pick_ref[b, :, k * width : (k + 1) * width] = hit.astype(jnp.bfloat16)
        return carry

    lax.fori_loop(0, owned, picks, 0)


def settle_own(pieces, owned, sizes):
    counts, places, width, note_rows = sizes
    order = pieces[0].shape[1]
    near = places * width
    narrow = jax.ShapeDtypeStruct((owned, order, near), jnp.bfloat16)
    return pl.pallas_call(
        functools.partial(settle_kernel, (counts, places, width, note_rows)),
        out_shape=[narrow, narrow],
        in_specs=[whole()] * 2,
        out_specs=[whole()] * 2,
        scratch_shapes=[
            pltpu.VMEM((2 * note_rows, width), jnp.float32),
            pltpu.VMEM((2 * note_rows, LANES), jnp.int32),
            pltpu.VMEM((owned, round_up(places, 8), width), jnp.float32),
        ],
        cost_estimate=pl.CostEstimate(
            flops=0, bytes_accessed=8 * owned * order * near, transcendentals=0
        ),
        compiler_params=pltpu.CompilerParams(vmem_limit_bytes=VMEM_LIMIT),
        name="settle_own",
    )(*pieces)


def first_kernel(dims, tables, *refs):
    counts, width, note_rows, parts, part = dims
    held = refs[:parts]
    refs = refs[parts:]
    pieces, near_ref, pick_ref, x_ref, z_ref, out = refs[:2], *refs[2:4], *refs[5:8]
    owned = x_ref.shape[0]
    notes, facts, stage, part_sems, stage_sems = refs[8:]
    my_col = lax.axis_index("col")
    copies = []
    for k, (sides, sources) in enumerate(tables):
        col = jnp.int32(0)
        for c, source in enumerate(sources):
            col = jnp.where(my_col == c, jnp.int32(source), col)
        start = pl.multiple_of(col * part, part)
        for at, side in enumerate(sides):
            copies.append(
                pltpu.make_async_copy(
                    held[k].at[pl.ds(at * owned, owned)],
                    (x_ref, z_ref)[side].at[:, pl.ds(start, part), :],
                    part_sems.at[2 * k + at],
                )
            )
            copies[-1].start()
    read_notes(pieces, notes, facts)
    for copy in copies:
        copy.wait()
    spans = [
        (piece, note_rows, first, count)
        for piece, count, first in zip(pieces, counts, (0, note_rows))
    ]
    weights = (x_ref, z_ref, near_ref, pick_ref)
    tiles_of(spans, width, notes, facts, weights, out, stage, stage_sems)


def first_tiles(held, pieces, near_weights, out, tables, sizes):
    counts, places, width, note_rows = sizes
    parts = len(held)
    owned = out.shape[0]
    part, order = held[0].shape[1:]
    near = places * width
    slots = 2 * side_by_side(counts)
    square = jax.ShapeDtypeStruct((owned, order, order), jnp.bfloat16)
    return pl.pallas_call(
        functools.partial(first_kernel, (counts, width, note_rows, parts, part), tables),
        out_shape=[square, square, jax.ShapeDtypeStruct(out.shape, out.dtype)],
        in_specs=[whole(pl.ANY)] * parts + [whole()] * 4 + [whole(pl.ANY)],
        out_specs=[whole()] * 2 + [whole(pl.ANY)],
        input_output_aliases={parts + 4: 2},
        scratch_shapes=[
            pltpu.VMEM((2 * note_rows, width), jnp.float32),
            pltpu.VMEM((2 * note_rows, LANES), jnp.int32),
            pltpu.VMEM((slots, width, near), jnp.float32),
            pltpu.SemaphoreType.DMA((2 * parts,)),
            pltpu.SemaphoreType.DMA((slots,)),
        ],
        cost_estimate=cost(sum(counts), order, width, near),
        compiler_params=pltpu.CompilerParams(vmem_limit_bytes=VMEM_LIMIT),
        name="first_tiles",
    )(*held, *pieces, *near_weights, out)


def next_kernel(spans, width, noted, count, *refs):
    pieces, weights = refs[:count], refs[count : count + 4]
    out, notes, facts, stage, stage_sems = refs[count + 5 :]
    read_notes(pieces[:noted], notes, facts)
    spans = [(pieces[k], base, first, groups) for k, base, first, groups in spans]
    tiles_of(spans, width, notes, facts, weights, out, stage, stage_sems)


def next_tiles(pieces, noted, spans, weights, out, sizes):
    counts, places, width, note_rows = sizes
    order = weights[0].shape[1]
    near = out.shape[2]
    count = len(pieces)
    slots = 2 * side_by_side([span[3] for span in spans])
    return pl.pallas_call(
        functools.partial(next_kernel, spans, width, noted, count),
        out_shape=jax.ShapeDtypeStruct(out.shape, out.dtype),
        in_specs=[whole()] * (count + 4) + [whole(pl.ANY)],
        out_specs=whole(pl.ANY),
        input_output_aliases={count + 4: 0},
        scratch_shapes=[
            pltpu.VMEM((noted * note_rows, width), jnp.float32),
            pltpu.VMEM((noted * note_rows, LANES), jnp.int32),
            pltpu.VMEM((slots, width, near), jnp.float32),
            pltpu.SemaphoreType.DMA((slots,)),
        ],
        cost_estimate=cost(sum(span[3] for span in spans), order, width, near),
        compiler_params=pltpu.CompilerParams(vmem_limit_bytes=VMEM_LIMIT),
        name="next_tiles",
    )(*pieces, *weights, out)


def body(basis, row_index, group_slot, x_blocks, zinv_blocks):
    row_count = lax.axis_size("row")
    col_count = lax.axis_size("col")
    groups, order, width = basis.shape
    owned = x_blocks.shape[0]
    places = GMAX // col_count
    capacity = (groups + row_count - 1) // row_count
    low = groups - (row_count - 2) * capacity
    early = 2 if 0 < low < groups else row_count
    low = low if early == 2 else groups // 2
    counts = (low, groups - low)
    note_rows = round_up(max(counts), 16)
    sizes = (counts, places, width, note_rows)

    ring = ring_order(col_count)
    place_of = {col: k for k, col in enumerate(ring)}
    ahead = [(ring[k], ring[(k + 1) % col_count]) for k in range(col_count)]
    behind = [(there, here) for here, there in ahead]
    full_steps = (col_count - 1) // 2
    split = col_count % 2 == 0 and col_count > 1

    def whose(offset):
        return [ring[(place_of[col] + offset) % col_count] for col in range(col_count)]

    bins = pack(group_slot, row_index, basis, row_count, capacity, owned)
    got = [bins[0]]
    for turn in range(1, row_count):
        pairs = [(k, partner(k, turn, row_count)) for k in range(row_count)]
        got.append(lax.ppermute(bins[turn], "row", pairs))
    own = [compact(got[:early], capacity, width, 0, counts[0], note_rows)]
    pairs_of = (ahead, behind)

    def both_ways(moving):
        return [lax.ppermute(moving[way], "col", pairs_of[way]) for way in range(2)]

    shape = (owned, GMAX * width, places * width)
    blocks = list(range(owned))
    parts = [jnp.concatenate([x_blocks, zinv_blocks], axis=0)]
    sides = [(0, 1)]
    held = list(parts)
    tables = [(side, whose(0)) for side in sides]
    going = [[part, part] for part in parts]
    out = None
    first = None
    for step in range(1, full_steps + 1):
        if step == 2:
            going, bins = lax.optimization_barrier((going, bins))
        if step == 3:
            going, got = lax.optimization_barrier((going, got))
        for k in range(len(parts)):
            going[k] = both_ways(going[k])
            for way, sign in enumerate((-1, 1)):
                held.append(going[k][way])
                tables.append((sides[k], whose(sign * step)))
        if step == 1:
            out = blank_tiles(shape, blocks[: owned // 2], going[-1])
        if step == max(full_steps - 1, 1):
            out = blank_tiles(shape, blocks[owned // 2 :], going[-1], out)
    if out is None:
        out = blank_tiles(shape, blocks, [])
    if full_steps:
        first = both_ways([own[0], own[0]])
        going, first, out = lax.optimization_barrier((going, first, out))
    if split:
        last = [going[0][0][:owned], going[0][1][owned:]]
        held += both_ways(last)
        tables += [((0,), whose(full_steps + 1)), ((1,), whose(full_steps + 1))]
    own.append(compact(got, capacity, width, counts[0], counts[1], note_rows))
    settled, _ = lax.optimization_barrier((own, going))
    near, pick = settle_own(settled, owned, sizes)

    streams = [[own[half], own[half]] for half in range(2)]
    arrived = []
    weights = None

    def advance(out, weights):
        if weights is None:
            x_full, z_full, out = first_tiles(held, own, (near, pick), out, tables, sizes)
            return out, (x_full, z_full, near, pick)
        pieces, noted, spans = arrived.pop(0)
        return next_tiles(pieces, noted, spans, weights, out, sizes), weights

    sent = 0
    for step in range(1, full_steps + 1):
        for half in range(2):
            moving = streams[half]
            if sent == 2:
                moving, near, pick = lax.optimization_barrier((moving, near, pick))
            if sent >= 3:
                if weights is None:
                    out, weights = advance(out, weights)
                out, weights = advance(out, weights)
                moving, out = lax.optimization_barrier((moving, out))
            moving = first if sent == 0 else both_ways(moving)
            streams[half] = moving
            spans = [(k, note_rows, k * note_rows, counts[half]) for k in range(2)]
            arrived.append((moving, 2, spans))
            sent += 1
    if split:
        for half in range(2):
            part = counts[half] // 2
            cut = note_rows + part * width
            moving = streams[half]
            if weights is None:
                out, weights = advance(out, weights)
            if arrived:
                out, weights = advance(out, weights)
                moving, out = lax.optimization_barrier((moving, out))
            moving = both_ways([moving[0][:cut], moving[1][cut:]])
            spans = [(0, note_rows, 0, part), (1, 0, part, counts[half] - part)]
            arrived.append((moving, 1, spans))
    if weights is None:
        out, weights = advance(out, weights)
    while arrived:
        out, weights = advance(out, weights)
    return out


def solution(mesh):
    placed = (
        P(("row", "col"), None, None),
        P(("row", "col"), None),
        P(("row", "col")),
        P("row", "col", None),
        P("row", "col", None),
    )
    return jax.shard_map(
        body, mesh=mesh, in_specs=placed, out_specs=P("row", None, "col"), check_vma=False
    )
```

time: 151 us -> 136 us (0.901)
  Pallas kernels: 74.7 us -> 61.4 us
  waiting for transfers between devices: 47.5 us -> 38.8 us
  starting transfers between devices: 25.3 us -> 30 us
  local copies, waits for them, and re-layouts: 2.72 us -> 4.62 us
    pallas_call x6 -> x14, Pallas kernels: 72.4 us -> 59 us  [the longest x8 36.8 us: next_tiles(): pl.pallas_call(functools.partial(next_kernel, spans, width, noted, count)...]
    ppermute x25 -> x27, waiting for transfers between devices: 47.5 us -> 38.8 us  [the longest x24 33.5 us: both_ways(): return [lax.ppermute(moving[way], 'col', pairs_of[way]) for way in range(2)]]
    ppermute x25 -> x27, starting transfers between devices: 25.3 us -> 30 us  [the longest x24 28 us: both_ways(): return [lax.ppermute(moving[way], 'col', pairs_of[way]) for way in range(2)]]
    unnamed x10 -> x7, local copies, waits for them, and re-layouts: 2.64 us -> 3.57 us
  transfers between devices with their start and end apart: 25 -> 27, of which waited for: 12 -> 15; matrix products, arithmetic and copies ran while one was open for 0% -> 0% of each run, Pallas kernels for 43% -> 43%
where the time goes in v2:
time: 136 us; the launch traced here: 135 us
  Pallas kernels  61.4 us (45%)
  waiting for transfers between devices  38.8 us (29%)
  starting transfers between devices  30 us (22%)
  local copies, waits for them, and re-layouts  4.62 us (3%)
    pallas_call x8, Pallas kernels, next_tiles(): pl.pallas_call(functools.partial(next_kernel, spans, width, noted, count)...  36.8 us
    ppermute x24, waiting for transfers between devices, both_ways(): return [lax.ppermute(moving[way], 'col', pairs_of[way]) for way in range(2)]  33.5 us
    ppermute x24, starting transfers between devices, both_ways(): return [lax.ppermute(moving[way], 'col', pairs_of[way]) for way in range(2)]  28 us
    pallas_call x2, Pallas kernels, blank_tiles(): pl.pallas_call(functools.partial(blank_kernel, blocks), out_shape=jax.Sha...  9.46 us
    pallas_call x1, Pallas kernels, first_tiles(): pl.pallas_call(functools.partial(first_kernel, (counts, width, note_rows,...  7.75 us
    ppermute x3, waiting for transfers between devices, body(): got.append(lax.ppermute(bins[turn], 'row', pairs))  5.3 us
    unnamed x7, local copies, waits for them, and re-layouts  3.57 us
  transfers between devices with their start and end apart: 27, of which 15 were waited for; matrix products, arithmetic and copies ran while one was open for 0% of the time, Pallas kernels for 43%

profile of v2, /device:TPU:0, one launch (start us, length us, event | category | flops | bytes accessed | tf_op | source)
XLA Modules:
  0.0 135.3 jit_solution(10989485852772612678)
XLA Ops:
  1.9 3.0 %collective-permute-start = (bf16[24,32,256]{2,1,0:T(8,128)(2,1)S(1)}, bf16[24,32,256]{2,1,0:T(8,128)(2,1)S(1)}, u32[]{:S(2)}, u32[]{:S(2)}) collective-permute-start(bf16[24,32,256]{2,1,0:T(8,128)(2,1)S(1)} %constant_dynamic-update-slice_fusion.refs_0_), channel_id=1, source_target_pairs={{1,3},{3,5},{5,7},{7,6},{6,4},{4,2},{2,0},{0,1},{9,11},{11,13},{13... | collective-permute-start | bytes 1179656 | tf_op jit(solution)/shard_map/ppermute | solution.py:494
  7.7 2.4 %pack.1 = (bf16[656,256]{1,0:T(8,128)(2,1)S(1)}, bf16[656,256]{1,0:T(8,128)(2,1)S(1)}, bf16[656,256]{1,0:T(8,128)(2,1)S(1)}, bf16[656,256]{1,0:T(8,128)(2,1)S(1)}) custom-call(s32[18]{0:T(128)S(1)} %copy-done.2, s32[18,128]{1,0:T(8,128)S(1)} %copy-done.1, bf16[18,256,128]{2,1,0:T(8,128)(2,1)S(1)} %copy-done), custom_call_target="tpu_custom_call" | custom-call | tf_op jit(solution)/shard_map/pack/pallas_call | solution.py:98
  10.1 1.9 %collective-permute-start.5 = (bf16[656,256]{1,0:T(8,128)(2,1)S(1)}, bf16[656,256]{1,0:T(8,128)(2,1)S(1)}, u32[]{:S(2)}, u32[]{:S(2)}) collective-permute-start(bf16[656,256]{1,0:T(8,128)(2,1)S(1)} %get-tuple-element.50), channel_id=1, source_target_pairs={{0,16},{8,24},{16,0},{24,8},{1,17},{9,25},{17,1},{25,9},{2,18},{10... | collective-permute-start | bytes 1007624 | tf_op jit(solution)/shard_map/ppermute | solution.py:489
  12.0 2.0 %collective-permute-done.refs_0_.refs_1_ = bf16[24,32,256]{2,1,0:T(8,128)(2,1)S(1)} collective-permute-done((bf16[24,32,256]{2,1,0:T(8,128)(2,1)S(1)}, bf16[24,32,256]{2,1,0:T(8,128)(2,1)S(1)}, u32[]{:S(2)}, u32[]{:S(2)}) %collective-permute-start) | collective-permute-done | bytes 393248 | tf_op jit(solution)/shard_map/ppermute | solution.py:494
  18.5 1.6 %collective-permute-start.11 = (bf16[1040,256]{1,0:T(8,128)(2,1)S(1)}, bf16[1040,256]{1,0:T(8,128)(2,1)S(1)}, u32[]{:S(2)}, u32[]{:S(2)}) collective-permute-start(bf16[1040,256]{1,0:T(8,128)(2,1)S(1)} %compact.3.refs_0_.refs_9_), channel_id=1, source_target_pairs={{1,3},{3,5},{5,7},{7,6},{6,4},{4,2},{2,0},{0,1},{9,11},{11,13},{13... | collective-permute-start | bytes 1597448 | tf_op jit(solution)/shard_map/ppermute | solution.py:494
  20.5 2.3 %collective-permute-start.12 = (bf16[1040,256]{1,0:T(8,128)(2,1)S(1)}, bf16[1040,256]{1,0:T(8,128)(2,1)S(1)}, u32[]{:S(2)}, u32[]{:S(2)}) collective-permute-start(bf16[1040,256]{1,0:T(8,128)(2,1)S(1)} %compact.3.refs_0_.refs_9_), channel_id=1, source_target_pairs={{3,1},{5,3},{7,5},{6,7},{4,6},{2,4},{0,2},{1,0},{11,9},{13,11},{15... | collective-permute-start | bytes 1597448 | tf_op jit(solution)/shard_map/ppermute | solution.py:494
  22.8 4.9 %collective-permute-done.6.refs_3_ = bf16[656,256]{1,0:T(8,128)(2,1)S(1)} collective-permute-done((bf16[656,256]{1,0:T(8,128)(2,1)S(1)}, bf16[656,256]{1,0:T(8,128)(2,1)S(1)}, u32[]{:S(2)}, u32[]{:S(2)}) %collective-permute-start.6) | collective-permute-done | bytes 335904 | tf_op jit(solution)/shard_map/ppermute | solution.py:489
  29.1 1.7 %collective-permute-start.9 = (bf16[24,32,256]{2,1,0:T(8,128)(2,1)S(1)}, bf16[24,32,256]{2,1,0:T(8,128)(2,1)S(1)}, u32[]{:S(2)}, u32[]{:S(2)}) collective-permute-start(bf16[24,32,256]{2,1,0:T(8,128)(2,1)S(1)} %collective-permute-done.2.refs_0_.refs_3_), channel_id=1, source_target_pairs={{1,3},{3,5},{5,7},{7,6},{6,4},{4,2},{2,0},{0,1},{9,11},{11,13},{13... | collective-permute-start | bytes 1179656 | tf_op jit(solution)/shard_map/ppermute | solution.py:494
  30.8 4.7 %blank_tiles.2.refs_2_ = f32[12,2048,256]{2,1,0:T(8,128)} custom-call(bf16[24,32,256]{2,1,0:T(8,128)(2,1)S(1)} %collective-permute-done.refs_0_.refs_1_, bf16[24,32,256]{2,1,0:T(8,128)(2,1)S(1)} %collective-permute-done.1.refs_1_.refs_2_), custom_call_target="tpu_custom_call" | custom-call | bytes 12582912 | tf_op jit(solution)/shard_map/blank_tiles/pallas_call | solution.py:289
  35.6 4.7 %blank_tiles.3.refs_13_ = f32[12,2048,256]{2,1,0:T(8,128)} custom-call(bf16[24,32,256]{2,1,0:T(8,128)(2,1)S(1)} %collective-permute-done.2.refs_0_.refs_3_, bf16[24,32,256]{2,1,0:T(8,128)(2,1)S(1)} %collective-permute-done.3.refs_1_.refs_4_, f32[12,2048,256]{2,1,0:T(8,128)} %blank_tiles.2.refs_2_), custom_call_target="tpu_custom_call", output_to_operand_aliasing={{}: (2, {})} | custom-call | bytes 12582912 | tf_op jit(solution)/shard_map/blank_tiles/pallas_call | solution.py:289
  40.3 6.0 %collective-permute-done.10.refs_6_ = bf16[24,32,256]{2,1,0:T(8,128)(2,1)S(1)} collective-permute-done((bf16[24,32,256]{2,1,0:T(8,128)(2,1)S(1)}, bf16[24,32,256]{2,1,0:T(8,128)(2,1)S(1)}, u32[]{:S(2)}, u32[]{:S(2)}) %collective-permute-start.10) | collective-permute-done | bytes 393248 | tf_op jit(solution)/shard_map/ppermute | solution.py:494
  46.3 1.6 %collective-permute-start.13 = (bf16[12,32,256]{2,1,0:T(8,128)(2,1)S(1)}, bf16[12,32,256]{2,1,0:T(8,128)(2,1)S(1)}, u32[]{:S(2)}, u32[]{:S(2)}) collective-permute-start(bf16[12,32,256]{2,1,0:T(8,128)(2,1)S(1)} %slice.18), channel_id=1, source_target_pairs={{1,3},{3,5},{5,7},{7,6},{6,4},{4,2},{2,0},{0,1},{9,11},{11,13},{13... | collective-permute-start | bytes 589832 | tf_op jit(solution)/shard_map/ppermute | solution.py:494
  49.8 1.6 %collective-permute-start.7 = (bf16[1296,256]{1,0:T(8,128)(2,1)S(1)}, bf16[1296,256]{1,0:T(8,128)(2,1)S(1)}, u32[]{:S(2)}, u32[]{:S(2)}) collective-permute-start(bf16[1296,256]{1,0:T(8,128)(2,1)S(1)} %compact.2.refs_1_.refs_10_), channel_id=1, source_target_pairs={{1,3},{3,5},{5,7},{7,6},{6,4},{4,2},{2,0},{0,1},{9,11},{11,13},{13... | collective-permute-start | bytes 1990664 | tf_op jit(solution)/shard_map/ppermute | solution.py:494
  51.9 2.7 %settle_own.1 = (bf16[12,256,256]{2,1,0:T(8,128)(2,1)S(1)}, bf16[12,256,256]{2,1,0:T(8,128)(2,1)S(1)}) custom-call(bf16[1040,256]{1,0:T(8,128)(2,1)S(1)} %compact.3.refs_0_.refs_9_, bf16[1296,256]{1,0:T(8,128)(2,1)S(1)} %compact.2.refs_1_.refs_10_), custom_call_target="tpu_custom_call" | custom-call | bytes 6291456 | tf_op jit(solution)/shard_map/settle_own/pallas_call | solution.py:350
  54.7 1.6 %collective-permute-start.17 = (bf16[1040,256]{1,0:T(8,128)(2,1)S(1)}, bf16[1040,256]{1,0:T(8,128)(2,1)S(1)}, u32[]{:S(2)}, u32[]{:S(2)}) collective-permute-start(bf16[1040,256]{1,0:T(8,128)(2,1)S(1)} %collective-permute-done.11.refs_0_), channel_id=1, source_target_pairs={{1,3},{3,5},{5,7},{7,6},{6,4},{4,2},{2,0},{0,1},{9,11},{11,13},{13... | collective-permute-start | bytes 1597448 | tf_op jit(solution)/shard_map/ppermute | solution.py:494
  56.7 7.8 %first_tiles.1 = (bf16[12,256,256]{2,1,0:T(8,128)(2,1)S(1)}, bf16[12,256,256]{2,1,0:T(8,128)(2,1)S(1)}, f32[12,2048,256]{2,1,0:T(8,128)}) custom-call(bf16[24,32,256]{2,1,0:T(8,128)(2,1)S(1)} %constant_dynamic-update-slice_fusion.refs_0_, bf16[24,32,256]{2,1,0:T(8,128)(2,1)S(1)} %collective-permute-done.refs_0_.refs_1_, ...), custom_call_target="tpu_custom_call", output_to_operand_aliasing={{2}: (13, {})} | custom-call | flops 3623878656 | bytes 3538944 | tf_op jit(solution)/shard_map/first_tiles/pallas_call | solution.py:410
  64.5 4.8 %next_tiles.8.refs_6_ = f32[12,2048,256]{2,1,0:T(8,128)} custom-call(bf16[1040,256]{1,0:T(8,128)(2,1)S(1)} %collective-permute-done.11.refs_0_, bf16[1040,256]{1,0:T(8,128)(2,1)S(1)} %collective-permute-done.12.refs_1_, bf16[12,256,256]{2,1,0:T(8,128)(2,1)S(1)} %get-tuple-element.71.refs_2_, ...), custom_call_target="tpu_custom_call", output_to_operand_aliasing={{}: (6, {})} | custom-call | flops 3221225472 | bytes 3145728 | tf_op jit(solution)/shard_map/next_tiles/pallas_call | solution.py:443
  72.0 5.6 %next_tiles.9.refs_6_ = f32[12,2048,256]{2,1,0:T(8,128)} custom-call(bf16[1296,256]{1,0:T(8,128)(2,1)S(1)} %collective-permute-done.7.refs_0_, bf16[1296,256]{1,0:T(8,128)(2,1)S(1)} %collective-permute-done.8.refs_1_, bf16[12,256,256]{2,1,0:T(8,128)(2,1)S(1)} %get-tuple-element.71.refs_2_, ...), custom_call_target="tpu_custom_call", output_to_operand_aliasing={{}: (6, {})} | custom-call | flops 4026531840 | bytes 3932160 | tf_op jit(solution)/shard_map/next_tiles/pallas_call | solution.py:443
  77.6 2.2 %collective-permute-done.17.refs_0_ = bf16[1040,256]{1,0:T(8,128)(2,1)S(1)} collective-permute-done((bf16[1040,256]{1,0:T(8,128)(2,1)S(1)}, bf16[1040,256]{1,0:T(8,128)(2,1)S(1)}, u32[]{:S(2)}, u32[]{:S(2)}) %collective-permute-start.17) | collective-permute-done | bytes 532512 | tf_op jit(solution)/shard_map/ppermute | solution.py:494
  79.8 1.6 %collective-permute-done.18.refs_1_ = bf16[1040,256]{1,0:T(8,128)(2,1)S(1)} collective-permute-done((bf16[1040,256]{1,0:T(8,128)(2,1)S(1)}, bf16[1040,256]{1,0:T(8,128)(2,1)S(1)}, u32[]{:S(2)}, u32[]{:S(2)}) %collective-permute-start.18) | collective-permute-done | bytes 532512 | tf_op jit(solution)/shard_map/ppermute | solution.py:494
  83.4 4.7 %next_tiles.10.refs_6_ = f32[12,2048,256]{2,1,0:T(8,128)} custom-call(bf16[1040,256]{1,0:T(8,128)(2,1)S(1)} %collective-permute-done.17.refs_0_, bf16[1040,256]{1,0:T(8,128)(2,1)S(1)} %collective-permute-done.18.refs_1_, bf16[12,256,256]{2,1,0:T(8,128)(2,1)S(1)} %get-tuple-element.71.refs_2_, ...), custom_call_target="tpu_custom_call", output_to_operand_aliasing={{}: (6, {})} | custom-call | flops 3221225472 | bytes 3145728 | tf_op jit(solution)/shard_map/next_tiles/pallas_call | solution.py:443
  88.2 5.8 %collective-permute-done.15.refs_0_ = bf16[1296,256]{1,0:T(8,128)(2,1)S(1)} collective-permute-done((bf16[1296,256]{1,0:T(8,128)(2,1)S(1)}, bf16[1296,256]{1,0:T(8,128)(2,1)S(1)}, u32[]{:S(2)}, u32[]{:S(2)}) %collective-permute-start.15) | collective-permute-done | bytes 663584 | tf_op jit(solution)/shard_map/ppermute | solution.py:494
  94.0 1.6 %collective-permute-done.16.refs_1_ = bf16[1296,256]{1,0:T(8,128)(2,1)S(1)} collective-permute-done((bf16[1296,256]{1,0:T(8,128)(2,1)S(1)}, bf16[1296,256]{1,0:T(8,128)(2,1)S(1)}, u32[]{:S(2)}, u32[]{:S(2)}) %collective-permute-start.16) | collective-permute-done | bytes 663584 | tf_op jit(solution)/shard_map/ppermute | solution.py:494
  97.6 5.6 %next_tiles.11.refs_6_ = f32[12,2048,256]{2,1,0:T(8,128)} custom-call(bf16[1296,256]{1,0:T(8,128)(2,1)S(1)} %collective-permute-done.15.refs_0_, bf16[1296,256]{1,0:T(8,128)(2,1)S(1)} %collective-permute-done.16.refs_1_, bf16[12,256,256]{2,1,0:T(8,128)(2,1)S(1)} %get-tuple-element.71.refs_2_, ...), custom_call_target="tpu_custom_call", output_to_operand_aliasing={{}: (6, {})} | custom-call | flops 4026531840 | bytes 3932160 | tf_op jit(solution)/shard_map/next_tiles/pallas_call | solution.py:443
  103.2 2.2 %collective-permute-done.21.refs_0_ = bf16[1040,256]{1,0:T(8,128)(2,1)S(1)} collective-permute-done((bf16[1040,256]{1,0:T(8,128)(2,1)S(1)}, bf16[1040,256]{1,0:T(8,128)(2,1)S(1)}, u32[]{:S(2)}, u32[]{:S(2)}) %collective-permute-start.21) | collective-permute-done | bytes 532512 | tf_op jit(solution)/shard_map/ppermute | solution.py:494
  107.0 1.6 %collective-permute-start.25 = (bf16[528,256]{1,0:T(8,128)(2,1)S(1)}, bf16[528,256]{1,0:T(8,128)(2,1)S(1)}, u32[]{:S(2)}, u32[]{:S(2)}) collective-permute-start(bf16[528,256]{1,0:T(8,128)(2,1)S(1)} %slice.22), channel_id=1, source_target_pairs={{1,3},{3,5},{5,7},{7,6},{6,4},{4,2},{2,0},{0,1},{9,11},{11,13},{13... | collective-permute-start | bytes 811016 | tf_op jit(solution)/shard_map/ppermute | solution.py:494
  109.2 4.8 %next_tiles.12.refs_6_ = f32[12,2048,256]{2,1,0:T(8,128)} custom-call(bf16[1040,256]{1,0:T(8,128)(2,1)S(1)} %collective-permute-done.21.refs_0_, bf16[1040,256]{1,0:T(8,128)(2,1)S(1)} %collective-permute-done.22.refs_1_, bf16[12,256,256]{2,1,0:T(8,128)(2,1)S(1)} %get-tuple-element.71.refs_2_, ...), custom_call_target="tpu_custom_call", output_to_operand_aliasing={{}: (6, {})} | custom-call | flops 3221225472 | bytes 3145728 | tf_op jit(solution)/shard_map/next_tiles/pallas_call | solution.py:443
  113.9 5.7 %collective-permute-done.19.refs_0_ = bf16[1296,256]{1,0:T(8,128)(2,1)S(1)} collective-permute-done((bf16[1296,256]{1,0:T(8,128)(2,1)S(1)}, bf16[1296,256]{1,0:T(8,128)(2,1)S(1)}, u32[]{:S(2)}, u32[]{:S(2)}) %collective-permute-start.19) | collective-permute-done | bytes 663584 | tf_op jit(solution)/shard_map/ppermute | solution.py:494
  121.2 1.6 %collective-permute-start.23 = (bf16[656,256]{1,0:T(8,128)(2,1)S(1)}, bf16[656,256]{1,0:T(8,128)(2,1)S(1)}, u32[]{:S(2)}, u32[]{:S(2)}) collective-permute-start(bf16[656,256]{1,0:T(8,128)(2,1)S(1)} %slice.20), channel_id=1, source_target_pairs={{1,3},{3,5},{5,7},{7,6},{6,4},{4,2},{2,0},{0,1},{9,11},{11,13},{13... | collective-permute-start | bytes 1007624 | tf_op jit(solution)/shard_map/ppermute | solution.py:494
  123.7 5.6 %next_tiles.13.refs_6_ = f32[12,2048,256]{2,1,0:T(8,128)} custom-call(bf16[1296,256]{1,0:T(8,128)(2,1)S(1)} %collective-permute-done.19.refs_0_, bf16[1296,256]{1,0:T(8,128)(2,1)S(1)} %collective-permute-done.20.refs_1_, bf16[12,256,256]{2,1,0:T(8,128)(2,1)S(1)} %get-tuple-element.71.refs_2_, ...), custom_call_target="tpu_custom_call", output_to_operand_aliasing={{}: (6, {})} | custom-call | flops 4026531840 | bytes 3932160 | tf_op jit(solution)/shard_map/next_tiles/pallas_call | solution.py:443
  129.3 2.7 %next_tiles.14.refs_6_ = f32[12,2048,256]{2,1,0:T(8,128)} custom-call(bf16[528,256]{1,0:T(8,128)(2,1)S(1)} %collective-permute-done.25.refs_0_, bf16[512,256]{1,0:T(8,128)(2,1)S(1)} %collective-permute-done.26.refs_1_, bf16[12,256,256]{2,1,0:T(8,128)(2,1)S(1)} %get-tuple-element.71.refs_2_, ...), custom_call_target="tpu_custom_call", output_to_operand_aliasing={{}: (6, {})} | custom-call | flops 1610612736 | bytes 1572864 | tf_op jit(solution)/shard_map/next_tiles/pallas_call | solution.py:443
  132.0 3.1 %next_tiles.15 = f32[12,2048,256]{2,1,0:T(8,128)} custom-call(bf16[656,256]{1,0:T(8,128)(2,1)S(1)} %collective-permute-done.23.refs_0_, bf16[640,256]{1,0:T(8,128)(2,1)S(1)} %collective-permute-done.24.refs_1_, bf16[12,256,256]{2,1,0:T(8,128)(2,1)S(1)} %get-tuple-element.71.refs_2_, ...), custom_call_target="tpu_custom_call", output_to_operand_aliasing={{}: (6, {})} | custom-call | flops 2013265920 | bytes 1966080 | tf_op jit(solution)/shard_map/next_tiles/pallas_call | solution.py:443
  (51 shorter events, 25.1 us)
Async XLA Ops:
  1.9 12.2 %collective-permute-start = (bf16[24,32,256]{2,1,0:T(8,128)(2,1)S(1)}, bf16[24,32,256]{2,1,0:T(8,128)(2,1)S(1)}, u32[]{:S(2)}, u32[]{:S(2)}) collective-permute-start(bf16[24,32,256]{2,1,0:T(8,128)(2,1)S(1)} %constant_dynamic-update-slice_fusion.refs_0_), channel_id=1, source_target_pairs={{1,3},{3,5},{5,7},{7,6},{6,4},{4,2},{2,0},{0,1},{9,11},{11,13},{13... | collective-permute-start | bytes 1179656 | tf_op jit(solution)/shard_map/ppermute | solution.py:494
  4.9 10.6 %collective-permute-start.1 = (bf16[24,32,256]{2,1,0:T(8,128)(2,1)S(1)}, bf16[24,32,256]{2,1,0:T(8,128)(2,1)S(1)}, u32[]{:S(2)}, u32[]{:S(2)}) collective-permute-start(bf16[24,32,256]{2,1,0:T(8,128)(2,1)S(1)} %constant_dynamic-update-slice_fusion.refs_0_), channel_id=1, source_target_pairs={{3,1},{5,3},{7,5},{6,7},{4,6},{2,4},{0,2},{1,0},{11,9},{13,11},{15... | collective-permute-start | bytes 1179656 | tf_op jit(solution)/shard_map/ppermute | solution.py:494
  5.0 1.3 copy-start
  6.3 0.7 copy-start.1
  7.0 0.7 copy-start.2
  10.0 7.5 %collective-permute-start.4 = (bf16[656,256]{1,0:T(8,128)(2,1)S(1)}, bf16[656,256]{1,0:T(8,128)(2,1)S(1)}, u32[]{:S(2)}, u32[]{:S(2)}) collective-permute-start(bf16[656,256]{1,0:T(8,128)(2,1)S(1)} %get-tuple-element.49), channel_id=1, source_target_pairs={{0,8},{8,0},{16,24},{24,16},{1,9},{9,1},{17,25},{25,17},{2,10},{10... | collective-permute-start | bytes 1007624 | tf_op jit(solution)/shard_map/ppermute | solution.py:489
  10.1 10.4 %collective-permute-start.5 = (bf16[656,256]{1,0:T(8,128)(2,1)S(1)}, bf16[656,256]{1,0:T(8,128)(2,1)S(1)}, u32[]{:S(2)}, u32[]{:S(2)}) collective-permute-start(bf16[656,256]{1,0:T(8,128)(2,1)S(1)} %get-tuple-element.50), channel_id=1, source_target_pairs={{0,16},{8,24},{16,0},{24,8},{1,17},{9,25},{17,1},{25,9},{2,18},{10... | collective-permute-start | bytes 1007624 | tf_op jit(solution)/shard_map/ppermute | solution.py:489
  15.5 12.2 %collective-permute-start.2 = (bf16[24,32,256]{2,1,0:T(8,128)(2,1)S(1)}, bf16[24,32,256]{2,1,0:T(8,128)(2,1)S(1)}, u32[]{:S(2)}, u32[]{:S(2)}) collective-permute-start(bf16[24,32,256]{2,1,0:T(8,128)(2,1)S(1)} %collective-permute-done.refs_0_.refs_1_), channel_id=1, source_target_pairs={{1,3},{3,5},{5,7},{7,6},{6,4},{4,2},{2,0},{0,1},{9,11},{11,13},{13... | collective-permute-start | bytes 1179656 | tf_op jit(solution)/shard_map/ppermute | solution.py:494
  17.1 11.7 %collective-permute-start.3 = (bf16[24,32,256]{2,1,0:T(8,128)(2,1)S(1)}, bf16[24,32,256]{2,1,0:T(8,128)(2,1)S(1)}, u32[]{:S(2)}, u32[]{:S(2)}) collective-permute-start(bf16[24,32,256]{2,1,0:T(8,128)(2,1)S(1)} %collective-permute-done.1.refs_1_.refs_2_), channel_id=1, source_target_pairs={{3,1},{5,3},{7,5},{6,7},{4,6},{2,4},{0,2},{1,0},{11,9},{13,11},{15... | collective-permute-start | bytes 1179656 | tf_op jit(solution)/shard_map/ppermute | solution.py:494
  17.5 10.2 %collective-permute-start.6 = (bf16[656,256]{1,0:T(8,128)(2,1)S(1)}, bf16[656,256]{1,0:T(8,128)(2,1)S(1)}, u32[]{:S(2)}, u32[]{:S(2)}) collective-permute-start(bf16[656,256]{1,0:T(8,128)(2,1)S(1)} %get-tuple-element.51), channel_id=1, source_target_pairs={{0,24},{8,16},{16,8},{24,0},{1,25},{9,17},{17,9},{25,1},{2,26},{10... | collective-permute-start | bytes 1007624 | tf_op jit(solution)/shard_map/ppermute | solution.py:489
  18.5 21.8 %collective-permute-start.11 = (bf16[1040,256]{1,0:T(8,128)(2,1)S(1)}, bf16[1040,256]{1,0:T(8,128)(2,1)S(1)}, u32[]{:S(2)}, u32[]{:S(2)}) collective-permute-start(bf16[1040,256]{1,0:T(8,128)(2,1)S(1)} %compact.3.refs_0_.refs_9_), channel_id=1, source_target_pairs={{1,3},{3,5},{5,7},{7,6},{6,4},{4,2},{2,0},{0,1},{9,11},{11,13},{13... | collective-permute-start | bytes 1597448 | tf_op jit(solution)/shard_map/ppermute | solution.py:494
  20.5 19.8 %collective-permute-start.12 = (bf16[1040,256]{1,0:T(8,128)(2,1)S(1)}, bf16[1040,256]{1,0:T(8,128)(2,1)S(1)}, u32[]{:S(2)}, u32[]{:S(2)}) collective-permute-start(bf16[1040,256]{1,0:T(8,128)(2,1)S(1)} %compact.3.refs_0_.refs_9_), channel_id=1, source_target_pairs={{3,1},{5,3},{7,5},{6,7},{4,6},{2,4},{0,2},{1,0},{11,9},{13,11},{15... | collective-permute-start | bytes 1597448 | tf_op jit(solution)/shard_map/ppermute | solution.py:494
  28.8 17.5 %collective-permute-start.10 = (bf16[24,32,256]{2,1,0:T(8,128)(2,1)S(1)}, bf16[24,32,256]{2,1,0:T(8,128)(2,1)S(1)}, u32[]{:S(2)}, u32[]{:S(2)}) collective-permute-start(bf16[24,32,256]{2,1,0:T(8,128)(2,1)S(1)} %collective-permute-done.3.refs_1_.refs_4_), channel_id=1, source_target_pairs={{3,1},{5,3},{7,5},{6,7},{4,6},{2,4},{0,2},{1,0},{11,9},{13,11},{15... | collective-permute-start | bytes 1179656 | tf_op jit(solution)/shard_map/ppermute | solution.py:494
  29.1 17.2 %collective-permute-start.9 = (bf16[24,32,256]{2,1,0:T(8,128)(2,1)S(1)}, bf16[24,32,256]{2,1,0:T(8,128)(2,1)S(1)}, u32[]{:S(2)}, u32[]{:S(2)}) collective-permute-start(bf16[24,32,256]{2,1,0:T(8,128)(2,1)S(1)} %collective-permute-done.2.refs_0_.refs_3_), channel_id=1, source_target_pairs={{1,3},{3,5},{5,7},{7,6},{6,4},{4,2},{2,0},{0,1},{9,11},{11,13},{13... | collective-permute-start | bytes 1179656 | tf_op jit(solution)/shard_map/ppermute | solution.py:494
  46.3 10.0 %collective-permute-start.13 = (bf16[12,32,256]{2,1,0:T(8,128)(2,1)S(1)}, bf16[12,32,256]{2,1,0:T(8,128)(2,1)S(1)}, u32[]{:S(2)}, u32[]{:S(2)}) collective-permute-start(bf16[12,32,256]{2,1,0:T(8,128)(2,1)S(1)} %slice.18), channel_id=1, source_target_pairs={{1,3},{3,5},{5,7},{7,6},{6,4},{4,2},{2,0},{0,1},{9,11},{11,13},{13... | collective-permute-start | bytes 589832 | tf_op jit(solution)/shard_map/ppermute | solution.py:494
  48.0 8.8 %collective-permute-start.14 = (bf16[12,32,256]{2,1,0:T(8,128)(2,1)S(1)}, bf16[12,32,256]{2,1,0:T(8,128)(2,1)S(1)}, u32[]{:S(2)}, u32[]{:S(2)}) collective-permute-start(bf16[12,32,256]{2,1,0:T(8,128)(2,1)S(1)} %slice.19), channel_id=1, source_target_pairs={{3,1},{5,3},{7,5},{6,7},{4,6},{2,4},{0,2},{1,0},{11,9},{13,11},{15... | collective-permute-start | bytes 589832 | tf_op jit(solution)/shard_map/ppermute | solution.py:494
  49.8 19.4 %collective-permute-start.7 = (bf16[1296,256]{1,0:T(8,128)(2,1)S(1)}, bf16[1296,256]{1,0:T(8,128)(2,1)S(1)}, u32[]{:S(2)}, u32[]{:S(2)}) collective-permute-start(bf16[1296,256]{1,0:T(8,128)(2,1)S(1)} %compact.2.refs_1_.refs_10_), channel_id=1, source_target_pairs={{1,3},{3,5},{5,7},{7,6},{6,4},{4,2},{2,0},{0,1},{9,11},{11,13},{13... | collective-permute-start | bytes 1990664 | tf_op jit(solution)/shard_map/ppermute | solution.py:494
  51.5 18.5 %collective-permute-start.8 = (bf16[1296,256]{1,0:T(8,128)(2,1)S(1)}, bf16[1296,256]{1,0:T(8,128)(2,1)S(1)}, u32[]{:S(2)}, u32[]{:S(2)}) collective-permute-start(bf16[1296,256]{1,0:T(8,128)(2,1)S(1)} %compact.2.refs_1_.refs_10_), channel_id=1, source_target_pairs={{3,1},{5,3},{7,5},{6,7},{4,6},{2,4},{0,2},{1,0},{11,9},{13,11},{15... | collective-permute-start | bytes 1990664 | tf_op jit(solution)/shard_map/ppermute | solution.py:494
  54.7 25.1 %collective-permute-start.17 = (bf16[1040,256]{1,0:T(8,128)(2,1)S(1)}, bf16[1040,256]{1,0:T(8,128)(2,1)S(1)}, u32[]{:S(2)}, u32[]{:S(2)}) collective-permute-start(bf16[1040,256]{1,0:T(8,128)(2,1)S(1)} %collective-permute-done.11.refs_0_), channel_id=1, source_target_pairs={{1,3},{3,5},{5,7},{7,6},{6,4},{4,2},{2,0},{0,1},{9,11},{11,13},{13... | collective-permute-start | bytes 1597448 | tf_op jit(solution)/shard_map/ppermute | solution.py:494
  56.3 25.1 %collective-permute-start.18 = (bf16[1040,256]{1,0:T(8,128)(2,1)S(1)}, bf16[1040,256]{1,0:T(8,128)(2,1)S(1)}, u32[]{:S(2)}, u32[]{:S(2)}) collective-permute-start(bf16[1040,256]{1,0:T(8,128)(2,1)S(1)} %collective-permute-done.12.refs_1_), channel_id=1, source_target_pairs={{3,1},{5,3},{7,5},{6,7},{4,6},{2,4},{0,2},{1,0},{11,9},{13,11},{15... | collective-permute-start | bytes 1597448 | tf_op jit(solution)/shard_map/ppermute | solution.py:494
  70.0 24.0 %collective-permute-start.15 = (bf16[1296,256]{1,0:T(8,128)(2,1)S(1)}, bf16[1296,256]{1,0:T(8,128)(2,1)S(1)}, u32[]{:S(2)}, u32[]{:S(2)}) collective-permute-start(bf16[1296,256]{1,0:T(8,128)(2,1)S(1)} %collective-permute-done.7.refs_0_), channel_id=1, source_target_pairs={{1,3},{3,5},{5,7},{7,6},{6,4},{4,2},{2,0},{0,1},{9,11},{11,13},{13... | collective-permute-start | bytes 1990664 | tf_op jit(solution)/shard_map/ppermute | solution.py:494
  71.5 24.1 %collective-permute-start.16 = (bf16[1296,256]{1,0:T(8,128)(2,1)S(1)}, bf16[1296,256]{1,0:T(8,128)(2,1)S(1)}, u32[]{:S(2)}, u32[]{:S(2)}) collective-permute-start(bf16[1296,256]{1,0:T(8,128)(2,1)S(1)} %collective-permute-done.8.refs_1_), channel_id=1, source_target_pairs={{3,1},{5,3},{7,5},{6,7},{4,6},{2,4},{0,2},{1,0},{11,9},{13,11},{15... | collective-permute-start | bytes 1990664 | tf_op jit(solution)/shard_map/ppermute | solution.py:494
  81.4 24.0 %collective-permute-start.21 = (bf16[1040,256]{1,0:T(8,128)(2,1)S(1)}, bf16[1040,256]{1,0:T(8,128)(2,1)S(1)}, u32[]{:S(2)}, u32[]{:S(2)}) collective-permute-start(bf16[1040,256]{1,0:T(8,128)(2,1)S(1)} %collective-permute-done.17.refs_0_), channel_id=1, source_target_pairs={{1,3},{3,5},{5,7},{7,6},{6,4},{4,2},{2,0},{0,1},{9,11},{11,13},{13... | collective-permute-start | bytes 1597448 | tf_op jit(solution)/shard_map/ppermute | solution.py:494
  82.9 24.1 %collective-permute-start.22 = (bf16[1040,256]{1,0:T(8,128)(2,1)S(1)}, bf16[1040,256]{1,0:T(8,128)(2,1)S(1)}, u32[]{:S(2)}, u32[]{:S(2)}) collective-permute-start(bf16[1040,256]{1,0:T(8,128)(2,1)S(1)} %collective-permute-done.18.refs_1_), channel_id=1, source_target_pairs={{3,1},{5,3},{7,5},{6,7},{4,6},{2,4},{0,2},{1,0},{11,9},{13,11},{15... | collective-permute-start | bytes 1597448 | tf_op jit(solution)/shard_map/ppermute | solution.py:494
  95.6 24.0 %collective-permute-start.19 = (bf16[1296,256]{1,0:T(8,128)(2,1)S(1)}, bf16[1296,256]{1,0:T(8,128)(2,1)S(1)}, u32[]{:S(2)}, u32[]{:S(2)}) collective-permute-start(bf16[1296,256]{1,0:T(8,128)(2,1)S(1)} %collective-permute-done.15.refs_0_), channel_id=1, source_target_pairs={{1,3},{3,5},{5,7},{7,6},{6,4},{4,2},{2,0},{0,1},{9,11},{11,13},{13... | collective-permute-start | bytes 1990664 | tf_op jit(solution)/shard_map/ppermute | solution.py:494
  97.2 24.1 %collective-permute-start.20 = (bf16[1296,256]{1,0:T(8,128)(2,1)S(1)}, bf16[1296,256]{1,0:T(8,128)(2,1)S(1)}, u32[]{:S(2)}, u32[]{:S(2)}) collective-permute-start(bf16[1296,256]{1,0:T(8,128)(2,1)S(1)} %collective-permute-done.16.refs_1_), channel_id=1, source_target_pairs={{3,1},{5,3},{7,5},{6,7},{4,6},{2,4},{0,2},{1,0},{11,9},{13,11},{15... | collective-permute-start | bytes 1990664 | tf_op jit(solution)/shard_map/ppermute | solution.py:494
  107.0 22.2 %collective-permute-start.25 = (bf16[528,256]{1,0:T(8,128)(2,1)S(1)}, bf16[528,256]{1,0:T(8,128)(2,1)S(1)}, u32[]{:S(2)}, u32[]{:S(2)}) collective-permute-start(bf16[528,256]{1,0:T(8,128)(2,1)S(1)} %slice.22), channel_id=1, source_target_pairs={{1,3},{3,5},{5,7},{7,6},{6,4},{4,2},{2,0},{0,1},{9,11},{11,13},{13... | collective-permute-start | bytes 811016 | tf_op jit(solution)/shard_map/ppermute | solution.py:494
  108.7 20.6 %collective-permute-start.26 = (bf16[512,256]{1,0:T(8,128)(2,1)S(1)}, bf16[512,256]{1,0:T(8,128)(2,1)S(1)}, u32[]{:S(2)}, u32[]{:S(2)}) collective-permute-start(bf16[512,256]{1,0:T(8,128)(2,1)S(1)} %slice.23), channel_id=1, source_target_pairs={{3,1},{5,3},{7,5},{6,7},{4,6},{2,4},{0,2},{1,0},{11,9},{13,11},{15... | collective-permute-start | bytes 786440 | tf_op jit(solution)/shard_map/ppermute | solution.py:494
  121.2 10.7 %collective-permute-start.23 = (bf16[656,256]{1,0:T(8,128)(2,1)S(1)}, bf16[656,256]{1,0:T(8,128)(2,1)S(1)}, u32[]{:S(2)}, u32[]{:S(2)}) collective-permute-start(bf16[656,256]{1,0:T(8,128)(2,1)S(1)} %slice.20), channel_id=1, source_target_pairs={{1,3},{3,5},{5,7},{7,6},{6,4},{4,2},{2,0},{0,1},{9,11},{11,13},{13... | collective-permute-start | bytes 1007624 | tf_op jit(solution)/shard_map/ppermute | solution.py:494
  122.9 9.0 %collective-permute-start.24 = (bf16[640,256]{1,0:T(8,128)(2,1)S(1)}, bf16[640,256]{1,0:T(8,128)(2,1)S(1)}, u32[]{:S(2)}, u32[]{:S(2)}) collective-permute-start(bf16[640,256]{1,0:T(8,128)(2,1)S(1)} %slice.21), channel_id=1, source_target_pairs={{3,1},{5,3},{7,5},{6,7},{4,6},{2,4},{0,2},{1,0},{11,9},{13,11},{15... | collective-permute-start | bytes 983048 | tf_op jit(solution)/shard_map/ppermute | solution.py:494
